TPU v7x, 32 devices: a whole 2x2x4 slice. The times are simulated.
32 devices in a mesh: blk: 8 (over z, x), panel: 4 (over y, core).
Axes of the slice: x: 2, y: 2, z: 4, core: 2. Of those that a mesh axis runs over, the one named last changes fastest.
Arguments:
- points: float32 [128, 6144], P(None, 'blk'), may hold values from -40 to 40
- lengthscale: float32 [128], replicated, may hold values from 5.656854 to 22.627417
- noise_level: float32 [1], replicated, may hold values from 0.5 to 1.5
- right_sides: float32 [17, 6144], P(None, 'blk'), may hold values from -6 to 6
- pivots: int32 [256], P('panel'), may hold values from 0 to 6143, as said below
Outputs:
- solution: float32 [17, 6144], P(None, 'blk')
- residual: float32 [17, 6144], P(None, 'blk')
Inputs may be any that keep to these rules, and one draw needn't show every extreme that they name: `pivots`: 256 distinct point indices; 0 and 6143 are always among them.
All inputs are finite; a program needn't handle non-finite values.
Results may differ from a plain program's by a relative error of at most 0.0003.
Values sent between devices are 32-bit elements; how exact they have to be, the bound alone decides.
A program may use at most 128 MiB of HBM per device.

v0:
```python
import jax
import jax.numpy as jnp
from jax import lax
from jax.sharding import PartitionSpec as P

ITERS = 2


HIGH = lax.Precision.HIGHEST


def tile_from(left_pts, right_pts, right_sq):
    cross_terms = lax.dot_general(
        left_pts,
        right_pts,
        (((0,), (0,)), ((), ())),
        precision=HIGH,
        preferred_element_type=jnp.float32,
    )
    left_sq = jnp.sum(left_pts * left_pts, axis=0)
    return jnp.exp(-0.5 * (left_sq[:, None] + right_sq[None, :] - 2.0 * cross_terms))


def row_products(left_mat, right_mat):
    return lax.dot_general(
        left_mat,
        right_mat,
        (((1,), (1,)), ((), ())),
        precision=HIGH,
        preferred_element_type=jnp.float32,
    )


def curvature_of(direction, images):
    return lax.psum(jnp.sum(direction * images, axis=1), "blk")


def inner_of(residual, preconditioned):
    return lax.psum(jnp.sum(residual * preconditioned, axis=1), "blk")


def per_device(points, lengthscale, noise_level, right_sides, pivots):
    row_count = points.shape[1]
    panel_size = lax.axis_size("panel")
    quarter = row_count // panel_size
    panel_start = lax.axis_index("panel") * quarter
    noise = noise_level[0]
    scaled = points / lengthscale[:, None]
    local_sq = jnp.sum(scaled * scaled, axis=0)
    row_ids = lax.axis_index("blk") * row_count + lax.iota(jnp.int32, row_count)
    onehot = (pivots[:, None] == row_ids[None, :]).astype(jnp.float32)
    picked = lax.psum(row_products(onehot, scaled), "blk")
    panel_part = tile_from(picked.T, scaled, local_sq)
    pivot_all, panel_rows = (
        lax.all_gather(picked, "panel", axis=0, tiled=True),
        lax.all_gather(panel_part, "panel", axis=0, tiled=True),
    )
    pivot_cols = pivot_all.T
    inner_kernel = tile_from(pivot_cols, pivot_cols, jnp.sum(pivot_cols * pivot_cols, axis=0))
    gram, projected = lax.psum(
        (row_products(panel_rows, panel_rows), row_products(panel_rows, right_sides)), "blk"
    )
    factor = jnp.linalg.cholesky(noise * inner_kernel + gram)

    def precondition(resid, proj):
        coefficients = jax.scipy.linalg.cho_solve((factor, True), proj)
        return (
            resid
            - jnp.dot(
                coefficients.T, panel_rows, precision=HIGH, preferred_element_type=jnp.float32
            )
        ) / noise

    solution = jnp.zeros_like(right_sides)
    residual = right_sides
    direction = precondition(residual, projected)
    precond_norm = inner_of(residual, direction)
    for iteration in range(ITERS):
        is_last = iteration + 1 == ITERS
        dir_part = lax.dynamic_slice_in_dim(direction, panel_start, quarter, 1)
        point_part = lax.dynamic_slice_in_dim(scaled, panel_start, quarter, 1)
        kernel_tile = tile_from(
            lax.all_gather(point_part, "blk", axis=1, tiled=True), scaled, local_sq
        )
        partial_image = jnp.dot(
            lax.all_gather(dir_part, "blk", axis=1, tiled=True),
            kernel_tile,
            precision=HIGH,
            preferred_element_type=jnp.float32,
        )
        images = lax.psum(partial_image, "panel") + noise * direction
        if is_last:
            curvature_sum = curvature_of(direction, images)
        else:
            curvature_sum = curvature_of(direction, images)
        step_size = precond_norm / curvature_sum
        solution = solution + step_size[:, None] * direction
        residual = residual - step_size[:, None] * images
        if not is_last:
            projected = lax.psum(row_products(panel_rows, residual), "blk")
            preconditioned = precondition(residual, projected)
            new_norm = inner_of(residual, preconditioned)
            direction = preconditioned + (new_norm / precond_norm)[:, None] * direction
            precond_norm = new_norm
    return (solution, residual)


def solution(mesh):
    return jax.shard_map(
        per_device,
        mesh=mesh,
        in_specs=(P(None, "blk"), P(), P(), P(None, "blk"), P("panel")),
        out_specs=(P(None, "blk"), P(None, "blk")),
        check_vma=False,
    )
```

profile of v0, /device:TPU:0, one launch (start us, length us, event | category | flops | bytes accessed | tf_op | source)
XLA Modules:
  0.0 393.7 jit_solution(17954180448473896501)
XLA Ops:
  7.2 1.2 copy.15
  8.4 0.8 multiply_reduce_fusion.1
  9.2 1.0 fusion.11
  10.2 38.8 %psum.70 = f32[64,128]{1,0:T(8,128)S(1)} all-reduce(f32[64,128]{1,0:T(8,128)S(1)} %fusion.11), channel_id=1, replica_groups=mesh['blk'=8,'panel'=4] {'blk'}, use_global_device_ids=true, to_apply=%region_0.0 | all-reduce | flops 8192 | bytes 65536 | tf_op jit(solution)/shard_map/psum | solution.py:52
  49.1 0.6 fusion.7
  49.7 8.6 %all_gather.17 = f32[256,768]{1,0:T(8,128)S(1)} all-gather(f32[64,768]{1,0:T(8,128)S(1)} %fusion.7), channel_id=1, replica_groups=mesh['blk'=8,'panel'=4] {'panel'}, dimensions={0}, use_global_device_ids=true | all-gather | bytes 983040 | tf_op jit(solution)/shard_map/all_gather | solution.py:56
  58.3 1.5 fusion.41
  59.9 5.4 %all_gather.16 = f32[256,128]{1,0:T(8,128)S(1)} all-gather(f32[64,128]{1,0:T(8,128)S(1)} %psum.70), channel_id=1, replica_groups=mesh['blk'=8,'panel'=4] {'panel'}, dimensions={0}, use_global_device_ids=true | all-gather | bytes 163840 | tf_op jit(solution)/shard_map/all_gather | solution.py:55
  66.2 0.7 fusion.42
  66.9 33.1 %psum.72 = f32[256,17]{0,1:T(8,128)S(1)} all-reduce(f32[256,17]{0,1:T(8,128)S(1)} %fusion.42), channel_id=1, replica_groups=mesh['blk'=8,'panel'=4] {'blk'}, use_global_device_ids=true, to_apply=%region_9.10 | all-reduce | flops 4352 | bytes 34816 | tf_op jit(solution)/shard_map/psum | solution.py:60
  100.0 32.3 %all_gather.19 = f32[128,1536]{0,1:T(8,128)S(1)} all-gather(f32[128,192]{0,1:T(8,128)S(1)} %constant_dynamic-slice_fusion.1), channel_id=1, replica_groups=mesh['blk'=8,'panel'=4] {'blk'}, dimensions={1}, use_global_device_ids=true | all-gather | bytes 884736 | tf_op jit(solution)/shard_map/all_gather | solution.py:83
  132.2 0.3 multiply_reduce_fusion
  132.5 6.1 %multiply_exponential_fusion = f32[1536,768]{1,0:T(8,128)} fusion(f32[128,1536]{0,1:T(8,128)S(1)} %all_gather.19, f32[128,768]{0,1:T(8,128)S(1)} %get-tuple-element.32, f32[768]{0:T(1024)S(1)} %get-tuple-element.31, f32[1536]{0:T(1024)S(1)} %multiply_reduce_fusion), kind=kOutput, calls=%fused_computation.2 | convolution fusion | flops 1816657920 | bytes 5907456 | tf_op jit(solution)/shard_map/dot_general | solution.py:13
  138.6 1.4 fusion.4
  140.2 11.7 %cholesky.50 = f32[128,128]{1,0:T(8,128)S(1)} custom-call(f32[128,128]{1,0:T(8,128)S(1)} %cholesky.118), custom_call_target="Cholesky" | custom-call | tf_op jit(solution)/shard_map/jit(cholesky)/cholesky | solution.py:63
  151.9 9.8 %custom-call.16 = f32[1,128,128]{1,2,0:T(8,128)S(1)} custom-call(f32[1,128,128]{2,1,0:T(8,128)S(1)} %get-tuple-element.40), custom_call_target="InvertDiagBlocksLowerTriangular" | custom-call | tf_op jit(solution)/shard_map/jit(cholesky)/cholesky | solution.py:63
  161.8 0.2 constant_dynamic-update-slice_fusion
  162.0 0.3 convolution_subtract_fusion.2
  162.3 11.7 %cholesky.105 = f32[128,128]{1,0:T(8,128)S(1)} custom-call(f32[128,128]{1,0:T(8,128)S(1)} %convolution_subtract_fusion.2), custom_call_target="Cholesky" | custom-call | tf_op jit(solution)/shard_map/jit(cholesky)/cholesky | solution.py:63
  174.0 0.6 compare_reduce_fusion
  176.0 3.8 while.4
  176.0 0.6 fusion.78
  176.5 1.3 bitcast_dynamic-update-slice_fusion.2
  177.9 0.6 fusion.78
  178.4 1.3 bitcast_dynamic-update-slice_fusion.2
  179.7 19.9 %custom-call.18 = f32[2,128,128]{1,2,0:T(8,128)S(1)} custom-call(f32[2,128,128]{2,1,0:T(8,128)S(1)} %get-tuple-element.17), custom_call_target="InvertDiagBlocksLowerTriangular" | custom-call | tf_op jit(solution)/shard_map/jit(_cho_solve)/triangular_solve | solution.py:66
  199.8 0.2 convolution_subtract_fusion.6
  200.2 0.2 fusion.24
  200.4 0.2 convolution_subtract_fusion.5
  200.6 0.2 fusion.20
  200.8 0.5 fusion.9
  201.4 30.6 %all-gather = f32[8,192,17]{1,2,0:T(8,128)S(1)} all-gather(f32[1,192,17]{1,2,0:T(8,128)S(1)} %dynamic-slice_bitcast_fusion.1), channel_id=1, replica_groups=mesh['blk'=8,'panel'=4] {'blk'}, dimensions={0}, use_global_device_ids=true | all-gather | bytes 117504 | tf_op jit(solution)/shard_map/all_gather | solution.py:86
  232.2 4.7 %fusion.43 = f32[17,768]{1,0:T(8,128)S(1)} fusion(f32[1536,17]{0,1:T(8,128)S(1)} %reshape.62, f32[1536,768]{1,0:T(8,128)} %multiply_exponential_fusion), kind=kOutput, calls=%fused_computation.89 | convolution fusion | flops 240648192 | bytes 4875264 | tf_op jit(solution)/shard_map/dot_general | solution.py:85
  236.9 11.4 %psum.74 = f32[17,768]{1,0:T(8,128)S(1)} all-reduce(f32[17,768]{1,0:T(8,128)S(1)} %fusion.43), channel_id=1, replica_groups=mesh['blk'=8,'panel'=4] {'panel'}, use_global_device_ids=true, to_apply=%region_13.15 | all-reduce | flops 13056 | bytes 104448 | tf_op jit(solution)/shard_map/psum | solution.py:91
  248.5 17.1 %all-reduce.1 = (f32[17]{0:T(128)S(1)}, f32[17]{0:T(128)S(1)}) all-reduce(f32[17]{0:T(128)S(1)} %get-tuple-element.20, f32[17]{0:T(128)S(1)} %get-tuple-element.19), channel_id=1, replica_groups=mesh['blk'=8,'panel'=4] {'blk'}, use_global_device_ids=true, to_apply=%region_11.13 | all-reduce | flops 34 | bytes 272 | tf_op jit(solution)/shard_map/psum | solution.py:39
  265.7 0.7 fusion.44
  266.4 34.9 %psum.76 = f32[256,17]{0,1:T(8,128)S(1)} all-reduce(f32[256,17]{0,1:T(8,128)S(1)} %fusion.44), channel_id=1, replica_groups=mesh['blk'=8,'panel'=4] {'blk'}, use_global_device_ids=true, to_apply=%region_16.18 | all-reduce | flops 4352 | bytes 34816 | tf_op jit(solution)/shard_map/psum | solution.py:100
  301.5 0.2 convolution_subtract_fusion.4
  301.9 0.2 fusion.22
  302.1 0.2 convolution_subtract_fusion.3
  302.3 0.2 fusion.18
  302.5 0.6 multiply_reduce_fusion.4
  303.1 17.2 %psum.77 = f32[17]{0:T(128)S(1)} all-reduce(f32[17]{0:T(128)S(1)} %get-tuple-element.43), channel_id=1, replica_groups=mesh['blk'=8,'panel'=4] {'blk'}, use_global_device_ids=true, to_apply=%region_18.20 | all-reduce | flops 17 | bytes 136 | tf_op jit(solution)/shard_map/psum | solution.py:39
  320.5 30.6 %all-gather.1 = f32[8,192,17]{1,2,0:T(8,128)S(1)} all-gather(f32[1,192,17]{1,2,0:T(8,128)S(1)} %dynamic-slice_bitcast_fusion), channel_id=1, replica_groups=mesh['blk'=8,'panel'=4] {'blk'}, dimensions={0}, use_global_device_ids=true | all-gather | bytes 117504 | tf_op jit(solution)/shard_map/all_gather | solution.py:86
  351.3 4.7 %fusion.45 = f32[17,768]{1,0:T(8,128)S(1)} fusion(f32[1536,17]{0,1:T(8,128)S(1)} %reshape.64, f32[1536,768]{1,0:T(8,128)} %multiply_exponential_fusion), kind=kOutput, calls=%fused_computation.91 | convolution fusion | flops 240648192 | bytes 4875264 | tf_op jit(solution)/shard_map/dot_general | solution.py:85
  356.0 11.0 %psum.78 = f32[17,768]{1,0:T(8,128)S(1)} all-reduce(f32[17,768]{1,0:T(8,128)S(1)} %fusion.45), channel_id=1, replica_groups=mesh['blk'=8,'panel'=4] {'panel'}, use_global_device_ids=true, to_apply=%region_19.21 | all-reduce | flops 13056 | bytes 104448 | tf_op jit(solution)/shard_map/psum | solution.py:91
  367.1 19.0 %psum.79 = f32[17]{0:T(128)S(1)} all-reduce(f32[17]{0:T(128)S(1)} %multiply_reduce_fusion.3), channel_id=1, replica_groups=mesh['blk'=8,'panel'=4] {'blk'}, use_global_device_ids=true, to_apply=%region_21.23 | all-reduce | flops 17 | bytes 136 | tf_op jit(solution)/shard_map/psum | solution.py:35
  386.2 0.7 multiply_subtract_fusion
  (38 shorter events, 2.3 us)
Async XLA Ops:
  7.2 59.0 %copy-start = (f32[17,768]{1,0:T(8,128)S(1)}, f32[17,768]{1,0:T(8,128)}, u32[]{:S(2)}) copy-start(f32[17,768]{1,0:T(8,128)} %param.10) | copy-start | bytes 156676
  7.2 131.4 %all-reduce.4.cloned.1.call-start = ((), (), s32[]{:S(2)}) async-start(), calls=%async_computation | async-start | bytes 524288 | tf_op jit(solution)/shard_map/psum | solution.py:60
Sparse Core Ops, SparseCore 0:
  60.0 66.8 all-reduce.3
where the time goes:
time: 394 us
  blocking collectives  290 us (74%)
  other arithmetic  56.4 us (14%)
  matrix products  25.2 us (6%)
  between operations  16.2 us (4%)
  local copies, waits for them, and re-layouts  5.61 us (1%)
    all_gather x2, blocking collectives, per_device(): lax.all_gather(dir_part, 'blk', axis=1, tiled=True)  61.2 us
    psum x1, blocking collectives, per_device(): picked = lax.psum(row_products(onehot, scaled), 'blk')  38.8 us
    psum x1, blocking collectives, per_device(): projected = lax.psum(row_products(panel_rows, residual), 'blk')  34.9 us
    psum x2, blocking collectives, inner_of(): return lax.psum(jnp.sum(residual * preconditioned, axis=1), 'blk')  34.4 us
    another operation x6, other arithmetic, per_device(): factor = jnp.linalg.cholesky(noise * inner_kernel + gram)  33.9 us
    psum x1, blocking collectives, per_device(): lax.psum((row_products(panel_rows, panel_rows), row_products(panel_rows,...  33.1 us
    all_gather x1, blocking collectives, per_device(): lax.all_gather(point_part, 'blk', axis=1, tiled=True)  32.3 us
    psum x2, blocking collectives, per_device(): images = lax.psum(partial_image, 'panel') + noise * direction  22.4 us
  transfers between devices with their start and end apart: 1, of which 0 were waited for; matrix products, arithmetic and copies ran while one was open for 2% of the time, Pallas kernels for 0%

commit v1 on v0

v1 whole, which is shorter than its diff:
```python
import functools

import jax
import jax.numpy as jnp
from jax import lax
from jax.experimental import pallas as pl
from jax.experimental.pallas import tpu as pltpu
from jax.sharding import PartitionSpec as P

HIGH = lax.Precision.HIGHEST
VMEM = pl.BlockSpec(memory_space=pltpu.VMEM)
MESH = pl.DeviceIdType.MESH
VMEM_BYTES = 48 * 1024 * 1024


def dot(left, right, left_dim, right_dim):
    return lax.dot_general(
        left,
        right,
        (((left_dim,), (right_dim,)), ((), ())),
        precision=HIGH,
        preferred_element_type=jnp.float32,
    )


def gather_kernel(axis, size, count, *refs):
    ins, outs = refs[:count], refs[count : 2 * count]
    send_sem, recv_sem = refs[2 * count :]
    me = lax.axis_index(axis)
    barrier = pltpu.get_barrier_semaphore()
    for hop in range(1, size):
        pl.semaphore_signal(
            barrier, inc=1, device_id={axis: lax.rem(me + hop, size)}, device_id_type=MESH
        )
    pl.semaphore_wait(barrier, size - 1)

    def copy_of(item, hop, slot):
        return pltpu.make_async_remote_copy(
            src_ref=ins[item],
            dst_ref=outs[item].at[slot],
            send_sem=send_sem.at[item, hop],
            recv_sem=recv_sem.at[item, hop],
            device_id={axis: lax.rem(me + hop, size)},
            device_id_type=MESH,
        )

    for hop in range(size - 1, 0, -1):
        for item in range(count):
            copy_of(item, hop, me).start()
    for item in range(count):
        outs[item][me] = ins[item][...]
    for hop in range(1, size):
        for item in range(count):
            copy_of(item, hop, lax.rem(me + size - hop, size)).wait_recv()
    for hop in range(1, size):
        for item in range(count):
            copy_of(item, hop, me).wait_send()


def gather(arrays, axis, collective_id):
    size = lax.axis_size(axis)
    count = len(arrays)
    return pl.pallas_call(
        functools.partial(gather_kernel, axis, size, count),
        out_shape=[jax.ShapeDtypeStruct((size,) + a.shape, a.dtype) for a in arrays],
        in_specs=[VMEM] * count,
        out_specs=[VMEM] * count,
        scratch_shapes=[
            pltpu.SemaphoreType.DMA((count, size)),
            pltpu.SemaphoreType.DMA((count, size)),
        ],
        compiler_params=pltpu.CompilerParams(
            collective_id=collective_id, has_side_effects=True, vmem_limit_bytes=VMEM_BYTES
        ),
    )(*arrays)


def sum_kernel(axis, steps, count, *refs):
    ins, outs = refs[:count], refs[count : 2 * count]
    landed = refs[2 * count : 3 * count]
    send_sem, recv_sem = refs[3 * count :]
    me = lax.axis_index(axis)
    partners = [me + s * (1 - 2 * lax.rem(me // s, 2)) for s in steps]
    barrier = pltpu.get_barrier_semaphore()
    for partner in partners:
        pl.semaphore_signal(barrier, inc=1, device_id={axis: partner}, device_id_type=MESH)
    pl.semaphore_wait(barrier, len(steps))
    held = list(ins)
    for step, partner in enumerate(partners):
        copies = []
        for item in range(count):
            copy = pltpu.make_async_remote_copy(
                src_ref=held[item],
                dst_ref=landed[item].at[step],
                send_sem=send_sem.at[item, step],
                recv_sem=recv_sem.at[item, step],
                device_id={axis: partner},
                device_id_type=MESH,
            )
            copy.start()
            copies.append(copy)
        for item in range(count):
            copies[item].wait()
            outs[item][...] = held[item][...] + landed[item][step]
            held[item] = outs[item]


def sum_over(arrays, axis, collective_id):
    size = lax.axis_size(axis)
    steps = []
    while (1 << len(steps)) < size:
        steps.append(1 << len(steps))
    count = len(arrays)
    return pl.pallas_call(
        functools.partial(sum_kernel, axis, steps, count),
        out_shape=[jax.ShapeDtypeStruct(a.shape, a.dtype) for a in arrays],
        in_specs=[VMEM] * count,
        out_specs=[VMEM] * count,
        scratch_shapes=[pltpu.VMEM((len(steps),) + a.shape, a.dtype) for a in arrays]
        + [
            pltpu.SemaphoreType.DMA((count, len(steps))),
            pltpu.SemaphoreType.DMA((count, len(steps))),
        ],
        compiler_params=pltpu.CompilerParams(
            collective_id=collective_id, has_side_effects=True, vmem_limit_bytes=VMEM_BYTES
        ),
    )(*arrays)


def kern(left, left_sq, right, right_dim, right_sq):
    cross = dot(left, right, 1, right_dim)
    return jnp.exp(-0.5 * (left_sq[:, None] + right_sq[None, :] - 2.0 * cross))


def per_device(points, lengthscale, noise_level, right_sides, pivots):
    row_count = points.shape[1]
    vec = right_sides.shape[0]
    panel_size = lax.axis_size("panel")
    quarter = row_count // panel_size
    panel_start = lax.axis_index("panel") * quarter
    noise = noise_level[0]
    scaled = points / lengthscale[:, None]
    local_sq = jnp.sum(scaled * scaled, axis=0)
    row_ids = lax.axis_index("blk") * row_count + lax.iota(jnp.int32, row_count)
    onehot = (pivots[:, None] == row_ids[None, :]).astype(jnp.float32)
    picked = dot(onehot, scaled, 1, 1)

    def own_quarter(vectors):
        return lax.dynamic_slice_in_dim(vectors, panel_start, quarter, 1)

    def spread(stacked):
        return stacked.transpose(1, 0, 2).reshape(vec, -1)

    quarter_points, picks, rhs_parts = gather(
        [own_quarter(scaled).T, picked, own_quarter(right_sides)], "blk", 0
    )
    visit = quarter_points.reshape(-1, points.shape[0])
    visit_sq = jnp.sum(visit * visit, axis=1)
    rhs_q = spread(rhs_parts)
    (pivot_parts,) = gather([jnp.sum(picks, axis=0)], "panel", 1)
    pivot_rows = pivot_parts.reshape(-1, points.shape[0])
    pivot_sq = jnp.sum(pivot_rows * pivot_rows, axis=1)

    panel_q = kern(pivot_rows, pivot_sq, visit, 1, visit_sq)
    panel_own = kern(pivot_rows, pivot_sq, scaled, 0, local_sq)
    inner_kernel = kern(pivot_rows, pivot_sq, pivot_rows, 1, pivot_sq)
    tile = kern(visit, visit_sq, scaled, 0, local_sq)

    gram, proj = sum_over([dot(panel_q, panel_q, 1, 1), dot(rhs_q, panel_q, 1, 1)], "panel", 2)
    factor = jnp.linalg.cholesky(noise * inner_kernel + gram)

    def coefficients_of(projected):
        return jax.scipy.linalg.cho_solve((factor, True), projected.T).T

    def precondition(resid, coefficients, panel_rows):
        return (resid - dot(coefficients, panel_rows, 1, 0)) / noise

    coef = coefficients_of(proj)
    dir_q = precondition(rhs_q, coef, panel_q)
    dir_own = precondition(right_sides, coef, panel_own)
    (image_own,) = sum_over([dot(dir_q, tile, 1, 0)], "panel", 3)
    image_own = image_own + noise * dir_own
    (image_parts,) = gather([own_quarter(image_own)], "blk", 4)
    image_q = spread(image_parts)
    lanes = lax.broadcasted_iota(jnp.int32, (1, 128), 1)

    def pack(columns):
        packed = jnp.zeros((vec, 128), jnp.float32)
        for index, column in enumerate(columns):
            packed = jnp.where(lanes == index, column[:, None], packed)
        return packed

    image_proj, dots = sum_over(
        [
            dot(image_q, panel_q, 1, 1),
            pack([jnp.sum(rhs_q * dir_q, axis=1), jnp.sum(dir_q * image_q, axis=1)]),
        ],
        "panel",
        5,
    )
    norm, curvature = dots[:, 0], dots[:, 1]
    step = (norm / curvature)[:, None]
    coef = coefficients_of(proj - step * image_proj)
    resid_own = right_sides - step * image_own
    pre_q = precondition(rhs_q - step * image_q, coef, panel_q)
    pre_own = precondition(resid_own, coef, panel_own)
    (pre_image,) = sum_over([dot(pre_q, tile, 1, 0)], "panel", 6)
    pre_image = pre_image + noise * pre_own
    (dot_parts,) = gather(
        [
            pack(
                [
                    jnp.sum(resid_own * pre_own, axis=1),
                    jnp.sum(pre_own * pre_image, axis=1),
                    jnp.sum(pre_own * image_own + dir_own * pre_image, axis=1),
                ]
            )
        ],
        "blk",
        7,
    )
    dots = jnp.sum(dot_parts, axis=0)
    new_norm = dots[:, 0]
    ratio = new_norm / norm
    curvature = dots[:, 1] + ratio * (dots[:, 2] + ratio * curvature)
    last = (new_norm / curvature)[:, None]
    ratio = ratio[:, None]
    solution = step * dir_own + last * (pre_own + ratio * dir_own)
    residual = resid_own - last * (pre_image + ratio * image_own)
    return (solution, residual)


def solution(mesh):
    return jax.shard_map(
        per_device,
        mesh=mesh,
        in_specs=(P(None, "blk"), P(), P(), P(None, "blk"), P("panel")),
        out_specs=(P(None, "blk"), P(None, "blk")),
        check_vma=False,
    )
```

time: 394 us -> 182 us (0.46)
  blocking collectives: 290 us -> 0 us
  Pallas kernels: 0 us -> 81.7 us
  between operations: 16.2 us -> 3.05 us
  local copies, waits for them, and re-layouts: 5.61 us -> 11.8 us
    psum x8 -> x0, blocking collectives: 183 us -> none  [the longest x1 38.8 us: per_device(): picked = lax.psum(row_products(onehot, scaled), 'blk')]
    all_gather x5 -> x0, blocking collectives: 108 us -> none  [the longest x2 61.2 us: per_device(): lax.all_gather(dir_part, 'blk', axis=1, tiled=True)]
    pallas_call x0 -> x8, Pallas kernels: none -> 81.7 us  [the longest x4 54.5 us: gather(): pl.pallas_call(functools.partial(gather_kernel, axis, size, count), out_s...]
    dot_general x11 -> x14, matrix products: 22.5 us -> 20.6 us  [dot(): lax.dot_general(left, right, (((left_dim,), (right_dim,)), ((), ())), pre...]
  transfers between devices with their start and end apart: 1 -> 0, of which waited for: 0 -> 0; matrix products, arithmetic and copies ran while one was open for 2% -> 0% of each run, Pallas kernels for 0% -> 0%
where the time goes in v1:
time: 182 us
  Pallas kernels  81.7 us (45%)
  other arithmetic  59.7 us (33%)
  matrix products  25.6 us (14%)
  local copies, waits for them, and re-layouts  11.8 us (6%)
  between operations  3.05 us (2%)
    pallas_call x4, Pallas kernels, gather(): pl.pallas_call(functools.partial(gather_kernel, axis, size, count), out_s...  54.5 us
    another operation x6, other arithmetic, per_device(): factor = jnp.linalg.cholesky(noise * inner_kernel + gram)  34.2 us
    pallas_call x4, Pallas kernels, sum_over(): pl.pallas_call(functools.partial(sum_kernel, axis, steps, count), out_sha...  27.2 us
    another operation x4, other arithmetic, coefficients_of(): return jax.scipy.linalg.cho_solve((factor, True), projected.T).T  21.7 us
    dot_general x14, matrix products, dot(): lax.dot_general(left, right, (((left_dim,), (right_dim,)), ((), ())), pre...  20.6 us
    another operation x7, local copies, waits for them, and re-layouts, coefficients_of(): return jax.scipy.linalg.cho_solve((factor, True), projected.T).T  5.09 us
    unnamed x21, local copies, waits for them, and re-layouts  4.39 us

profile of v1, /device:TPU:0, one launch (start us, length us, event | category | flops | bytes accessed | tf_op | source)
XLA Modules:
  0.0 181.8 jit_solution(2322405016815532624)
XLA Ops:
  0.7 1.2 copy.11
  1.8 0.8 multiply_reduce_fusion.1
  2.8 0.3 fusion.16.refs_1_
  3.1 34.2 %shard_map.68 = (f32[8,192,128]{2,1,0:T(8,128)S(1)}, f32[8,64,128]{2,1,0:T(8,128)S(1)}, f32[8,17,192]{2,1,0:T(8,128)S(1)}) custom-call(f32[192,128]{1,0:T(8,128)S(1)} %dynamic-slice_bitcast_fusion.refs_0_, f32[64,128]{1,0:T(8,128)S(1)} %fusion.16.refs_1_, f32[17,192]{1,0:T(8,128)S(1)} %constant_dynamic-slice_fusion.2.refs_2_), custom_call_target="tpu_custom_call" | custom-call | tf_op jit(solution)/shard_map/pallas_call | solution.py:63
  37.4 4.5 %shard_map.69 = f32[4,64,128]{2,1,0:T(8,128)S(1)} custom-call(f32[64,128]{1,0:T(8,128)S(1)} %reduce_sum.90.refs_0_), custom_call_target="tpu_custom_call" | custom-call | tf_op jit(solution)/shard_map/pallas_call | solution.py:63
  42.1 0.4 multiply_reduce_fusion
  42.6 1.6 fusion.2
  44.4 1.3 fusion.48.refs_1_
  45.7 1.5 fusion.47.refs_0_
  47.2 10.7 %shard_map.70 = (f32[256,256]{1,0:T(8,128)S(1)}, f32[17,256]{1,0:T(8,128)S(1)}) custom-call(f32[256,256]{1,0:T(8,128)S(1)} %fusion.47.refs_0_, f32[17,256]{1,0:T(8,128)S(1)} %fusion.48.refs_1_), custom_call_target="tpu_custom_call" | custom-call | tf_op jit(solution)/shard_map/pallas_call | solution.py:114
  57.9 0.8 copy.14
  59.4 1.4 fusion.12
  60.8 0.8 copy.15
  61.6 1.0 fusion.15
  62.6 0.7 copy-done.8
  63.3 11.7 %cholesky.50 = f32[128,128]{1,0:T(8,128)S(1)} custom-call(f32[128,128]{1,0:T(8,128)S(1)} %cholesky.118), custom_call_target="Cholesky" | custom-call | tf_op jit(solution)/shard_map/jit(cholesky)/cholesky | solution.py:170
  75.1 10.0 %custom-call.16 = f32[1,128,128]{1,2,0:T(8,128)S(1)} custom-call(f32[1,128,128]{2,1,0:T(8,128)S(1)} %get-tuple-element.57), custom_call_target="InvertDiagBlocksLowerTriangular" | custom-call | tf_op jit(solution)/shard_map/jit(cholesky)/cholesky | solution.py:170
  85.0 1.0 constant_dynamic-update-slice_fusion
  86.1 1.1 convolution_subtract_fusion.4
  87.2 11.7 %cholesky.105 = f32[128,128]{1,0:T(8,128)S(1)} custom-call(f32[128,128]{1,0:T(8,128)S(1)} %convolution_subtract_fusion.4), custom_call_target="Cholesky" | custom-call | tf_op jit(solution)/shard_map/jit(cholesky)/cholesky | solution.py:170
  98.9 0.7 compare_reduce_fusion
  100.9 1.0 select_select_fusion
  102.0 5.0 %while.4 = (s32[]{:T(128)}, f32[256,256]{1,0:T(8,128)S(1)}, s32[2,2]{1,0:T(2,128)S(1)}, f32[2,128,128]{2,1,0:T(8,128)}, s32[]{:T(128)}) while((s32[]{:T(128)}, f32[256,256]{1,0:T(8,128)S(1)}, s32[2,2]{1,0:T(2,128)S(1)}, f32[2,128,128]{2,1,0:T(8,128)}, s32[]{:T(128)}) %tuple.41), condition=%wide.while_cond, body=%wide.while_body.sunk | while | flops 2 | bytes 132705 | solution.py:173
  102.0 0.6 fusion.88
  102.6 1.9 %bitcast_dynamic-update-slice_fusion.2 = f32[2,128,128]{2,1,0:T(8,128)} fusion(f32[2,128,128]{2,1,0:T(8,128)} %get-tuple-element.104, s32[]{:T(128)} %get-tuple-element.101, f32[256,256]{1,0:T(8,128)S(1)} %get-tuple-element.107, s32[]{:T(128)} %bitcast.81, s32[]{:T(128)} %bitcast.82), kind=kLoop, calls=%fused_computation.clone.1 | loop fusion | bytes 132608 | tf_op jit(solution)/shard_map/jit(_cho_solve) | solution.py:173
  104.5 0.6 fusion.88
  105.1 1.9 %bitcast_dynamic-update-slice_fusion.2 = f32[2,128,128]{2,1,0:T(8,128)} fusion(f32[2,128,128]{2,1,0:T(8,128)} %get-tuple-element.104, s32[]{:T(128)} %get-tuple-element.101, f32[256,256]{1,0:T(8,128)S(1)} %get-tuple-element.107, s32[]{:T(128)} %bitcast.81, s32[]{:T(128)} %bitcast.82), kind=kLoop, calls=%fused_computation.clone.1 | loop fusion | bytes 132608 | tf_op jit(solution)/shard_map/jit(_cho_solve) | solution.py:173
  107.0 20.7 %custom-call.18 = f32[2,128,128]{1,2,0:T(8,128)S(1)} custom-call(f32[2,128,128]{2,1,0:T(8,128)} %get-tuple-element.31), custom_call_target="InvertDiagBlocksLowerTriangular" | custom-call | tf_op jit(solution)/shard_map/jit(_cho_solve)/triangular_solve | solution.py:173
  128.1 0.3 fusion.30
  129.1 0.9 fusion.4
  130.0 4.7 %multiply_exponential_fusion = f32[1536,768]{1,0:T(8,128)S(1)} fusion(f32[1536,128]{1,0:T(8,128)S(1)} %bitcast.90, f32[128,768]{0,1:T(8,128)S(1)} %get-tuple-element.49, f32[768]{0:T(1024)S(1)} %get-tuple-element.48, f32[1536]{0:T(1024)S(1)} %add.132), kind=kOutput, calls=%fused_computation.2 | convolution fusion | flops 1816657920 | bytes 5907456 | tf_op jit(solution)/shard_map/dot_general | solution.py:17
  134.7 2.1 %copy-done = f32[1536,768]{1,0:T(8,128)} copy-done((f32[1536,768]{1,0:T(8,128)}, f32[1536,768]{1,0:T(8,128)S(1)}, u32[]{:S(2)}) %copy-start) | copy-done | bytes 4718616
  136.8 2.4 %fusion.49.refs_0_ = f32[17,768]{1,0:T(8,128)S(1)} fusion(f32[17,1536]{1,0:T(8,128)S(1)} %fusion.4, f32[1536,768]{1,0:T(8,128)S(1)} %multiply_exponential_fusion), kind=kOutput, calls=%fused_computation.108 | convolution fusion | flops 240648192 | bytes 4875264 | tf_op jit(solution)/shard_map/dot_general | solution.py:17
  139.2 5.8 %shard_map.71 = f32[17,768]{1,0:T(8,128)S(1)} custom-call(f32[17,768]{1,0:T(8,128)S(1)} %fusion.49.refs_0_), custom_call_target="tpu_custom_call" | custom-call | tf_op jit(solution)/shard_map/pallas_call | solution.py:114
  145.0 0.9 fusion.7
  145.9 0.5 multiply_add_fusion.2
  146.4 0.4 copy-done.2
  146.9 8.7 %shard_map.72 = f32[8,17,192]{2,1,0:T(8,128)S(1)} custom-call(f32[17,192]{1,0:T(8,128)S(1)} %constant_dynamic-slice_fusion.1.refs_0_), custom_call_target="tpu_custom_call" | custom-call | tf_op jit(solution)/shard_map/pallas_call | solution.py:63
  156.0 1.3 fusion.50.refs_0_
  157.3 4.9 %shard_map.73 = (f32[17,256]{1,0:T(8,128)S(1)}, f32[17,128]{1,0:T(8,128)S(1)}) custom-call(f32[17,256]{1,0:T(8,128)S(1)} %fusion.50.refs_0_, f32[17,128]{1,0:T(8,128)S(1)} %select_select_fusion.2.refs_1_), custom_call_target="tpu_custom_call" | custom-call | tf_op jit(solution)/shard_map/pallas_call | solution.py:114
  162.9 0.3 fusion.28
  163.2 0.4 fusion.27
  164.0 0.9 fusion.3
  164.9 2.3 %fusion.51.refs_0_ = f32[17,768]{1,0:T(8,128)S(1)} fusion(f32[17,1536]{1,0:T(8,128)S(1)} %fusion.3, f32[1536,768]{1,0:T(8,128)S(1)} %copy-done.1), kind=kOutput, calls=%fused_computation.110 | convolution fusion | flops 240648192 | bytes 4875264 | tf_op jit(solution)/shard_map/dot_general | solution.py:17
  167.3 5.8 %shard_map.74 = f32[17,768]{1,0:T(8,128)S(1)} custom-call(f32[17,768]{1,0:T(8,128)S(1)} %fusion.51.refs_0_), custom_call_target="tpu_custom_call" | custom-call | tf_op jit(solution)/shard_map/pallas_call | solution.py:114
  173.1 0.6 add_reduce_fusion
  173.8 7.0 %shard_map.75 = f32[8,17,128]{2,1,0:T(8,128)S(1)} custom-call(f32[17,128]{1,0:T(8,128)S(1)} %select_select_fusion.1.refs_0_), custom_call_target="tpu_custom_call" | custom-call | tf_op jit(solution)/shard_map/pallas_call | solution.py:63
  181.1 0.8 multiply_subtract_fusion
  (56 shorter events, 3.5 us)
Async XLA Ops:
  0.6 2.1 %copy-start.7 = (f32[17,768]{1,0:T(8,128)S(1)}, f32[17,768]{1,0:T(8,128)}, u32[]{:S(2)}) copy-start(f32[17,768]{1,0:T(8,128)} %param.10) | copy-start | bytes 156676
  0.6 2.2 %copy-start.9 = (s32[64]{0:T(128)S(1)}, s32[64]{0:T(128)}, u32[]{:S(2)}) copy-start(s32[64]{0:T(128)} %param.11) | copy-start | bytes 772
  62.6 0.7 copy-start.8
  98.9 2.0 %copy-start.6 = (f32[256,256]{1,0:T(8,128)}, f32[256,256]{1,0:T(8,128)S(1)}, u32[]{:S(2)}) copy-start(f32[256,256]{1,0:T(8,128)S(1)} %get-tuple-element.55) | copy-start | bytes 786436
  130.0 4.7 %copy-start.4 = (f32[17,1536]{1,0:T(8,128)}, f32[17,1536]{1,0:T(8,128)S(1)}, u32[]{:S(2)}) copy-start(f32[17,1536]{1,0:T(8,128)S(1)} %fusion.4) | copy-start | bytes 313348
  134.7 2.1 %copy-start = (f32[1536,768]{1,0:T(8,128)}, f32[1536,768]{1,0:T(8,128)S(1)}, u32[]{:S(2)}) copy-start(f32[1536,768]{1,0:T(8,128)S(1)} %multiply_exponential_fusion) | copy-start | bytes 14155780
  145.0 10.7 %copy-start.5 = (f32[17,1536]{1,0:T(8,128)S(1)}, f32[17,1536]{1,0:T(8,128)}, u32[]{:S(2)}) copy-start(f32[17,1536]{1,0:T(8,128)} %copy-done.4) | copy-start | bytes 313348
  145.9 0.9 copy-start.2
  155.7 9.2 %copy-start.1 = (f32[1536,768]{1,0:T(8,128)S(1)}, f32[1536,768]{1,0:T(8,128)}, u32[]{:S(2)}) copy-start(f32[1536,768]{1,0:T(8,128)} %copy-done) | copy-start | bytes 14155780
  164.9 8.2 %copy-start.3 = (f32[256,768]{1,0:T(8,128)S(1)}, f32[256,768]{1,0:T(8,128)}, u32[]{:S(2)}) copy-start(f32[256,768]{1,0:T(8,128)} %copy-done.2) | copy-start | bytes 2359300

commit v2 on v1

--- a/solution.py
+++ b/solution.py
@@ -127,6 +127,57 @@
     )(*arrays)
 
 
+def inverse_kernel(side, part, width, a_ref, out_ref):
+    sub = lax.broadcasted_iota(jnp.int32, (part, part), 0)
+    lane = lax.broadcasted_iota(jnp.int32, (part, part), 1)
+    head = lax.broadcasted_iota(jnp.int32, (1, part), 1)
+    out_ref[...] = a_ref[...]
+
+    def block_step(_, carry):
+        block = out_ref[:part, :part]
+        for first in range(0, part, width):
+            columns = [
+                jnp.broadcast_to(block[:, k : k + 1], (part, part))
+                for k in range(first, first + width)
+            ]
+            for index in range(width):
+                k = first + index
+                here = sub == k
+                column = columns[index]
+                scale = 1.0 / column[k : k + 1, :]
+                row = jnp.where(head == k, 1.0, block[k : k + 1, :]) * scale
+                factor = jnp.where(here, -1.0, column)
+                block = jnp.where(here | (lane == k), 0.0, block) - factor * row
+                for later in range(index + 1, width):
+                    entry = columns[later][k : k + 1, :] * scale
+                    columns[later] = jnp.where(here, 0.0, columns[later]) - factor * entry
+        left = out_ref[part:, :part]
+        right = dot(block, out_ref[:part, part:], 1, 0)
+        rest = out_ref[part:, part:] - dot(left, right, 1, 0)
+        side_part = -dot(left, block, 1, 0)
+        out_ref[...] = jnp.concatenate(
+            [
+                jnp.concatenate([rest, side_part], axis=1),
+                jnp.concatenate([right, block], axis=1),
+            ],
+            axis=0,
+        )
+        return carry
+
+    lax.fori_loop(0, side // part, block_step, 0)
+
+
+def inverse_of(matrix):
+    side = matrix.shape[0]
+    return pl.pallas_call(
+        functools.partial(inverse_kernel, side, 64, 8),
+        out_shape=jax.ShapeDtypeStruct(matrix.shape, matrix.dtype),
+        in_specs=[VMEM],
+        out_specs=VMEM,
+        compiler_params=pltpu.CompilerParams(vmem_limit_bytes=VMEM_BYTES),
+    )(matrix)
+
+
 def kern(left, left_sq, right, right_dim, right_sq):
     cross = dot(left, right, 1, right_dim)
     return jnp.exp(-0.5 * (left_sq[:, None] + right_sq[None, :] - 2.0 * cross))
@@ -167,10 +218,10 @@
     tile = kern(visit, visit_sq, scaled, 0, local_sq)
 
     gram, proj = sum_over([dot(panel_q, panel_q, 1, 1), dot(rhs_q, panel_q, 1, 1)], "panel", 2)
-    factor = jnp.linalg.cholesky(noise * inner_kernel + gram)
+    inverse = inverse_of(noise * inner_kernel + gram)
 
     def coefficients_of(projected):
-        return jax.scipy.linalg.cho_solve((factor, True), projected.T).T
+        return dot(projected, inverse, 1, 0)
 
     def precondition(resid, coefficients, panel_rows):
         return (resid - dot(coefficients, panel_rows, 1, 0)) / noise

time: 182 us -> 124 us (0.68)
  other arithmetic: 59.7 us -> 2.78 us
  Pallas kernels: 81.7 us -> 92.4 us
  local copies, waits for them, and re-layouts: 11.8 us -> 4.31 us
  matrix products: 25.6 us -> 22.8 us
    another operation x10 -> x0, other arithmetic: 55.9 us -> none  [the longest x6 34.2 us: per_device(): factor = jnp.linalg.cholesky(noise * inner_kernel + gram)]
    pallas_call x0 -> x1, Pallas kernels: none -> 10.6 us  [inverse_of(): pl.pallas_call(functools.partial(inverse_kernel, side, 64, 8), out_shape=...]
    another operation x9 -> x0, local copies, waits for them, and re-layouts: 5.12 us -> none  [the longest x7 5.09 us: coefficients_of(): return jax.scipy.linalg.cho_solve((factor, True), projected.T).T]
    another operation x14 -> x0, matrix products: 4.91 us -> none  [the longest x12 2.76 us: coefficients_of(): return jax.scipy.linalg.cho_solve((factor, True), projected.T).T]
    dot_general x14 -> x16, matrix products: 20.6 us -> 22.8 us  [dot(): lax.dot_general(left, right, (((left_dim,), (right_dim,)), ((), ())), pre...]
    unnamed x21 -> x11, local copies, waits for them, and re-layouts: 4.39 us -> 3.69 us
where the time goes in v2:
time: 124 us
  Pallas kernels  92.4 us (75%)
  matrix products  22.8 us (18%)
  local copies, waits for them, and re-layouts  4.31 us (3%)
  other arithmetic  2.78 us (2%)
  between operations  1.6 us (1%)
    pallas_call x4, Pallas kernels, gather(): pl.pallas_call(functools.partial(gather_kernel, axis, size, count), out_s...  54.5 us
    pallas_call x4, Pallas kernels, sum_over(): pl.pallas_call(functools.partial(sum_kernel, axis, steps, count), out_sha...  27.3 us
    dot_general x16, matrix products, dot(): lax.dot_general(left, right, (((left_dim,), (right_dim,)), ((), ())), pre...  22.8 us
    pallas_call x1, Pallas kernels, inverse_of(): pl.pallas_call(functools.partial(inverse_kernel, side, 64, 8), out_shape=...  10.6 us
    unnamed x11, local copies, waits for them, and re-layouts  3.69 us

profile of v2, /device:TPU:0, one launch (start us, length us, event | category | flops | bytes accessed | tf_op | source)
XLA Modules:
  0.0 123.9 jit_solution(10795072675207876526)
XLA Ops:
  0.6 0.0 copy-start.3
  0.6 0.0 copy-start.4
  0.7 1.2 copy.8
  1.8 0.8 multiply_reduce_fusion.1
  2.7 0.0 copy-done.3
  2.7 0.1 constant_dynamic-slice_fusion.1.refs_2_
  2.8 0.0 copy-done.4
  2.8 0.3 fusion.15.refs_1_
  3.1 34.2 %shard_map.68 = (f32[8,192,128]{2,1,0:T(8,128)S(1)}, f32[8,64,128]{2,1,0:T(8,128)S(1)}, f32[8,17,192]{2,1,0:T(8,128)S(1)}) custom-call(f32[192,128]{1,0:T(8,128)S(1)} %dynamic-slice_bitcast_fusion.refs_0_, f32[64,128]{1,0:T(8,128)S(1)} %fusion.15.refs_1_, f32[17,192]{1,0:T(8,128)S(1)} %constant_dynamic-slice_fusion.1.refs_2_), custom_call_target="tpu_custom_call" | custom-call | tf_op jit(solution)/shard_map/pallas_call | solution.py:63
  37.4 4.5 %shard_map.69 = f32[4,64,128]{2,1,0:T(8,128)S(1)} custom-call(f32[64,128]{1,0:T(8,128)S(1)} %reduce_sum.90.refs_0_), custom_call_target="tpu_custom_call" | custom-call | tf_op jit(solution)/shard_map/pallas_call | solution.py:63
  41.9 0.1 multiply_reduce_fusion.4
  42.1 0.1 add.103
  42.1 0.4 multiply_reduce_fusion
  42.5 0.1 add.105
  42.6 1.6 %fusion.2 = f32[256,1536]{1,0:T(8,128)S(1)} fusion(f32[256,128]{1,0:T(8,128)S(1)} %bitcast.45, f32[1536,128]{1,0:T(8,128)S(1)} %bitcast.43, f32[1536]{0:T(1024)S(1)} %add.105, f32[256]{0:T(256)S(1)} %add.103), kind=kOutput, calls=%fused_computation.4 | convolution fusion | flops 605552640 | bytes 2497536 | tf_op jit(solution)/shard_map/dot_general | solution.py:17
  44.3 0.1 reshape.53
  44.4 1.3 %fusion.29.refs_1_ = f32[17,256]{1,0:T(8,128)S(1)} fusion(f32[17,1536]{1,0:T(8,128)S(1)} %reshape.53, f32[256,1536]{1,0:T(8,128)S(1)} %fusion.2), kind=kOutput, calls=%fused_computation.63 | convolution fusion | flops 80216064 | bytes 1694720 | tf_op jit(solution)/shard_map/dot_general | solution.py:17
  45.7 1.4 %fusion.28.refs_0_ = f32[256,256]{1,0:T(8,128)S(1)} fusion(f32[256,1536]{1,0:T(8,128)S(1)} %fusion.2), kind=kOutput, calls=%fused_computation.62 | convolution fusion | flops 1207959552 | bytes 1835008 | tf_op jit(solution)/shard_map/dot_general | solution.py:17
  47.2 10.7 %shard_map.70 = (f32[256,256]{1,0:T(8,128)S(1)}, f32[17,256]{1,0:T(8,128)S(1)}) custom-call(f32[256,256]{1,0:T(8,128)S(1)} %fusion.28.refs_0_, f32[17,256]{1,0:T(8,128)S(1)} %fusion.29.refs_1_), custom_call_target="tpu_custom_call" | custom-call | tf_op jit(solution)/shard_map/pallas_call | solution.py:114
  58.5 0.4 fusion.12.a_ref
  59.0 10.6 %shard_map.71 = f32[256,256]{1,0:T(8,128)S(1)} custom-call(f32[256,256]{1,0:T(8,128)S(1)} %fusion.12.a_ref), custom_call_target="tpu_custom_call" | custom-call | tf_op jit(solution)/shard_map/pallas_call | solution.py:172
  69.6 0.2 fusion.30
  69.9 0.9 fusion.4
  70.7 4.7 %multiply_exponential_fusion = f32[1536,768]{1,0:T(8,128)S(1)} fusion(f32[1536,128]{1,0:T(8,128)S(1)} %bitcast.44, f32[128,768]{0,1:T(8,128)S(1)} %get-tuple-element.24, f32[768]{0:T(1024)S(1)} %get-tuple-element.23, f32[1536]{0:T(1024)S(1)} %add.105), kind=kOutput, calls=%fused_computation | convolution fusion | flops 1816657920 | bytes 5907456 | tf_op jit(solution)/shard_map/dot_general | solution.py:17
  75.4 0.0 copy-start
  75.4 2.1 %copy-done = f32[1536,768]{1,0:T(8,128)} copy-done((f32[1536,768]{1,0:T(8,128)}, f32[1536,768]{1,0:T(8,128)S(1)}, u32[]{:S(2)}) %copy-start) | copy-done | bytes 4718616
  77.5 2.4 %fusion.31.refs_0_ = f32[17,768]{1,0:T(8,128)S(1)} fusion(f32[17,1536]{1,0:T(8,128)S(1)} %fusion.4, f32[1536,768]{1,0:T(8,128)S(1)} %multiply_exponential_fusion), kind=kOutput, calls=%fused_computation.65 | convolution fusion | flops 240648192 | bytes 4875264 | tf_op jit(solution)/shard_map/dot_general | solution.py:17
  79.9 5.8 %shard_map.72 = f32[17,768]{1,0:T(8,128)S(1)} custom-call(f32[17,768]{1,0:T(8,128)S(1)} %fusion.31.refs_0_), custom_call_target="tpu_custom_call" | custom-call | tf_op jit(solution)/shard_map/pallas_call | solution.py:114
  85.7 0.9 fusion.7
  86.6 0.5 multiply_add_fusion.2
  87.1 0.4 copy-done.1
  87.5 0.1 constant_dynamic-slice_fusion.refs_0_
  87.6 8.7 %shard_map.73 = f32[8,17,192]{2,1,0:T(8,128)S(1)} custom-call(f32[17,192]{1,0:T(8,128)S(1)} %constant_dynamic-slice_fusion.refs_0_), custom_call_target="tpu_custom_call" | custom-call | tf_op jit(solution)/shard_map/pallas_call | solution.py:63
  96.4 0.1 reshape.56
  96.5 0.1 multiply_reduce_fusion.3
  96.6 0.1 select_select_fusion.1.refs_1_
  96.7 1.3 %fusion.32.refs_0_ = f32[17,256]{1,0:T(8,128)S(1)} fusion(f32[17,1536]{1,0:T(8,128)S(1)} %reshape.56, f32[256,1536]{1,0:T(8,128)S(1)} %fusion.2), kind=kOutput, calls=%fused_computation.66 | convolution fusion | flops 80216064 | bytes 1694720 | tf_op jit(solution)/shard_map/dot_general | solution.py:17
  98.0 4.9 %shard_map.74 = (f32[17,256]{1,0:T(8,128)S(1)}, f32[17,128]{1,0:T(8,128)S(1)}) custom-call(f32[17,256]{1,0:T(8,128)S(1)} %fusion.32.refs_0_, f32[17,128]{1,0:T(8,128)S(1)} %select_select_fusion.1.refs_1_), custom_call_target="tpu_custom_call" | custom-call | tf_op jit(solution)/shard_map/pallas_call | solution.py:114
  103.0 0.2 divide_reduce_fusion
  103.1 0.3 fusion.19
  103.4 1.1 fusion.3
  104.5 4.7 %fusion.33.refs_0_ = f32[17,768]{1,0:T(8,128)S(1)} fusion(f32[17,1536]{1,0:T(8,128)S(1)} %fusion.3, f32[1536,768]{1,0:T(8,128)} %copy-done), kind=kOutput, calls=%fused_computation.67 | convolution fusion | flops 240648192 | bytes 4875264 | tf_op jit(solution)/shard_map/dot_general | solution.py:17
  109.3 5.8 %shard_map.75 = f32[17,768]{1,0:T(8,128)S(1)} custom-call(f32[17,768]{1,0:T(8,128)S(1)} %fusion.33.refs_0_), custom_call_target="tpu_custom_call" | custom-call | tf_op jit(solution)/shard_map/pallas_call | solution.py:114
  115.1 0.6 add_reduce_fusion
  115.8 0.1 select_select_fusion.refs_0_
  115.8 7.0 %shard_map.76 = f32[8,17,128]{2,1,0:T(8,128)S(1)} custom-call(f32[17,128]{1,0:T(8,128)S(1)} %select_select_fusion.refs_0_), custom_call_target="tpu_custom_call" | custom-call | tf_op jit(solution)/shard_map/pallas_call | solution.py:63
  122.9 0.2 fusion.26
  123.1 0.8 multiply_subtract_fusion
  (11 shorter events, 0.2 us)
Async XLA Ops:
  0.6 2.1 %copy-start.3 = (f32[17,768]{1,0:T(8,128)S(1)}, f32[17,768]{1,0:T(8,128)}, u32[]{:S(2)}) copy-start(f32[17,768]{1,0:T(8,128)} %param.8) | copy-start | bytes 156676
  0.6 2.2 %copy-start.4 = (s32[64]{0:T(128)S(1)}, s32[64]{0:T(128)}, u32[]{:S(2)}) copy-start(s32[64]{0:T(128)} %param.9) | copy-start | bytes 772
  75.4 2.1 %copy-start = (f32[1536,768]{1,0:T(8,128)}, f32[1536,768]{1,0:T(8,128)S(1)}, u32[]{:S(2)}) copy-start(f32[1536,768]{1,0:T(8,128)S(1)} %multiply_exponential_fusion) | copy-start | bytes 14155780
  86.6 0.9 copy-start.1
  104.5 10.6 %copy-start.2 = (f32[256,768]{1,0:T(8,128)S(1)}, f32[256,768]{1,0:T(8,128)}, u32[]{:S(2)}) copy-start(f32[256,768]{1,0:T(8,128)} %copy-done.1) | copy-start | bytes 2359300

commit v3 on v2

--- a/solution.py
+++ b/solution.py
@@ -7,18 +7,19 @@
 from jax.experimental.pallas import tpu as pltpu
 from jax.sharding import PartitionSpec as P
 
-HIGH = lax.Precision.HIGHEST
+FULL = lax.Precision.HIGHEST
 VMEM = pl.BlockSpec(memory_space=pltpu.VMEM)
 MESH = pl.DeviceIdType.MESH
-VMEM_BYTES = 48 * 1024 * 1024
-
-
-def dot(left, right, left_dim, right_dim):
+VMEM_BYTES = 16 * 1024 * 1024
+LOOP_BYTES = 28 * 1024 * 1024
+
+
+def dot(left, right, left_dim, right_dim, precision=lax.Precision.HIGH):
     return lax.dot_general(
         left,
         right,
         (((left_dim,), (right_dim,)), ((), ())),
-        precision=HIGH,
+        precision=precision,
         preferred_element_type=jnp.float32,
     )
 
@@ -69,6 +70,120 @@
             pltpu.SemaphoreType.DMA((count, size)),
             pltpu.SemaphoreType.DMA((count, size)),
         ],
+        compiler_params=pltpu.CompilerParams(
+            collective_id=collective_id, has_side_effects=True, vmem_limit_bytes=VMEM_BYTES
+        ),
+    )(*arrays)
+
+
+def forward_kernel(axis, size, count, *refs):
+    ins, outs = refs[:count], refs[count : 2 * count]
+    up_send, up_recv, down_send, down_recv, pair_send, pair_recv = refs[2 * count :]
+    half = size // 2
+    me = lax.axis_index(axis)
+    place = me // 2
+    partner = me + 1 - 2 * lax.rem(me, 2)
+    has_above, has_below = place < half - 1, place > 0
+    barrier = pltpu.get_barrier_semaphore()
+
+    def greet(device):
+        pl.semaphore_signal(barrier, inc=1, device_id={axis: device}, device_id_type=MESH)
+
+    greet(partner)
+    pl.when(has_above)(lambda: greet(me + 2))
+    pl.when(has_below)(lambda: greet(me - 2))
+    pl.semaphore_wait(barrier, 1 + has_above.astype(jnp.int32) + has_below.astype(jnp.int32))
+
+    def copies(own, slot, sends, recvs, index, device):
+        return [
+            pltpu.make_async_remote_copy(
+                src_ref=ins[item] if own else outs[item].at[slot],
+                dst_ref=outs[item].at[slot],
+                send_sem=sends.at[item, index],
+                recv_sem=recvs.at[item, index],
+                device_id={axis: device},
+                device_id_type=MESH,
+            )
+            for item in range(count)
+        ]
+
+    def up(distance):
+        slot = me - 2 * (distance - 1)
+        return copies(distance == 1, slot, up_send, up_recv, distance, me + 2)
+
+    def down(distance):
+        slot = me + 2 * (distance - 1)
+        return copies(distance == 1, slot, down_send, down_recv, distance, me - 2)
+
+    def pair(shift):
+        index = abs(shift) if shift <= 0 else half - 1 + shift
+        return copies(shift == 0, me + 2 * shift, pair_send, pair_recv, index, partner)
+
+    def start(group):
+        for copy in group:
+            copy.start()
+
+    def arrived(group_of, slot, sends, recvs, index):
+        for copy in copies(False, slot, sends, recvs, index, group_of):
+            copy.wait_recv()
+
+    pl.when(has_above)(lambda: start(up(1)))
+    pl.when(has_below)(lambda: start(down(1)))
+    start(pair(0))
+    for item in range(count):
+        outs[item][me] = ins[item][...]
+    for distance in range(1, half):
+
+        @pl.when(place - distance >= 0)
+        def _():
+            arrived(partner, me - 2 * distance, up_send, up_recv, distance)
+            if distance < half - 1:
+                pl.when(has_above)(lambda: start(up(distance + 1)))
+            start(pair(-distance))
+
+        @pl.when(place + distance <= half - 1)
+        def _():
+            arrived(partner, me + 2 * distance, down_send, down_recv, distance)
+            if distance < half - 1:
+                pl.when(has_below)(lambda: start(down(distance + 1)))
+            start(pair(distance))
+
+    def sent(group):
+        for copy in group:
+            copy.wait_send()
+
+    def settle(shift):
+        index = abs(shift) if shift <= 0 else half - 1 + shift
+        arrived(partner, partner + 2 * shift, pair_send, pair_recv, index)
+        sent(pair(shift))
+
+    settle(0)
+    pl.when(has_above)(lambda: sent(up(1)))
+    pl.when(has_below)(lambda: sent(down(1)))
+    for distance in range(1, half):
+
+        @pl.when(place - distance >= 0)
+        def _():
+            settle(-distance)
+            if distance < half - 1:
+                pl.when(has_above)(lambda: sent(up(distance + 1)))
+
+        @pl.when(place + distance <= half - 1)
+        def _():
+            settle(distance)
+            if distance < half - 1:
+                pl.when(has_below)(lambda: sent(down(distance + 1)))
+
+
+def forward_gather(arrays, axis, collective_id):
+    size = lax.axis_size(axis)
+    count = len(arrays)
+    return pl.pallas_call(
+        functools.partial(forward_kernel, axis, size, count),
+        out_shape=[jax.ShapeDtypeStruct((size,) + a.shape, a.dtype) for a in arrays],
+        in_specs=[VMEM] * count,
+        out_specs=[VMEM] * count,
+        scratch_shapes=[pltpu.SemaphoreType.DMA((count, size))] * 6,
         compiler_params=pltpu.CompilerParams(
             collective_id=collective_id, has_side_effects=True, vmem_limit_bytes=VMEM_BYTES
         ),
@@ -152,9 +267,9 @@
                     entry = columns[later][k : k + 1, :] * scale
                     columns[later] = jnp.where(here, 0.0, columns[later]) - factor * entry
         left = out_ref[part:, :part]
-        right = dot(block, out_ref[:part, part:], 1, 0)
-        rest = out_ref[part:, part:] - dot(left, right, 1, 0)
-        side_part = -dot(left, block, 1, 0)
+        right = dot(block, out_ref[:part, part:], 1, 0, FULL)
+        rest = out_ref[part:, part:] - dot(left, right, 1, 0, FULL)
+        side_part = -dot(left, block, 1, 0, FULL)
         out_ref[...] = jnp.concatenate(
             [
                 jnp.concatenate([rest, side_part], axis=1),
@@ -179,8 +294,172 @@
 
 
 def kern(left, left_sq, right, right_dim, right_sq):
-    cross = dot(left, right, 1, right_dim)
+    cross = dot(left, right, 1, right_dim, FULL)
     return jnp.exp(-0.5 * (left_sq[:, None] + right_sq[None, :] - 2.0 * cross))
+
+
+def loop_kernel(size, panel_size, vec, quarter, *refs):
+    proj_ref, inverse_ref, rhs_parts, rhs_own, panel_parts, panel_own = refs[:6]
+    high_ref, low_ref, noise_ref, solution_ref, residual_ref = refs[6:11]
+    dir_parts, pre_parts, first_sum, second_sum, image_parts, dot_sum, last_sum = refs[11:18]
+    send_sem, recv_sem = refs[18:]
+    row, column = lax.axis_index("blk"), lax.axis_index("panel")
+    rank = proj_ref.shape[1]
+    barrier = pltpu.get_barrier_semaphore()
+    for hop in range(1, size):
+        pl.semaphore_signal(
+            barrier, inc=1, device_id={"blk": lax.rem(row + hop, size)}, device_id_type=MESH
+        )
+    for hop in range(1, panel_size):
+        pl.semaphore_signal(
+            barrier,
+            inc=1,
+            device_id={"panel": lax.rem(column + hop, panel_size)},
+            device_id_type=MESH,
+        )
+    noise = noise_ref[...]
+
+    def exchange(axis, buffer, phase):
+        me, count = (row, size) if axis == "blk" else (column, panel_size)
+
+        def copy_of(hop, slot):
+            return pltpu.make_async_remote_copy(
+                src_ref=buffer.at[slot],
+                dst_ref=buffer.at[slot],
+                send_sem=send_sem.at[phase, hop],
+                recv_sem=recv_sem.at[phase, hop],
+                device_id={axis: lax.rem(me + hop, count)},
+                device_id_type=MESH,
+            )
+
+        for hop in range(count - 1, 0, -1):
+            copy_of(hop, me).start()
+        for hop in range(1, count):
+            copy_of(hop, lax.rem(me + count - hop, count)).wait_recv()
+        for hop in range(1, count):
+            copy_of(hop, me).wait_send()
+
+    def total_of(buffer, count):
+        total = buffer[0]
+        for index in range(1, count):
+            total = total + buffer[index]
+        return total
+
+    def precondition(resid, coefficients, panel_rows):
+        return (resid - dot(coefficients, panel_rows, 1, 0, FULL)) / noise
+
+    def tile_product(parts):
+        product = jnp.zeros(rhs_own.shape, jnp.float32)
+        for index in range(size):
+            rows = pl.ds(index * quarter, quarter)
+            part = parts[index]
+            high = part.astype(jnp.bfloat16)
+            low = (part - high.astype(jnp.float32)).astype(jnp.bfloat16)
+            for left, right in ((high, high_ref), (low, high_ref), (high, low_ref)):
+                product = product + lax.dot_general(
+                    left,
+                    right[rows, :],
+                    (((1,), (0,)), ((), ())),
+                    preferred_element_type=jnp.float32,
+                )
+        return product
+
+    def row_sum(left, right):
+        return jnp.sum(left * right, axis=1, keepdims=True)
+
+    lanes = lax.broadcasted_iota(jnp.int32, (vec, 128), 1)
+
+    def pack(columns):
+        packed = jnp.zeros((vec, 128), jnp.float32)
+        for index, value in enumerate(columns):
+            packed = jnp.where(lanes == index, value, packed)
+        return packed
+
+    coef = dot(proj_ref[...], inverse_ref[...], 1, 0, FULL)
+    for index in range(size):
+        dir_parts[index] = precondition(rhs_parts[index], coef, panel_parts[index])
+    first_sum[column] = tile_product(dir_parts)
+    pl.semaphore_wait(barrier, size + panel_size - 2)
+    exchange("panel", first_sum, 0)
+    dir_own = precondition(rhs_own[...], coef, panel_own[...])
+    image_own = total_of(first_sum, panel_size) + noise * dir_own
+    for index in range(panel_size):
+
+        @pl.when(column == index)
+        def _():
+            image_parts[row] = image_own[:, index * quarter : (index + 1) * quarter]
+
+    exchange("blk", image_parts, 1)
+    image_proj = jnp.zeros((vec, rank), jnp.float32)
+    norm = jnp.zeros((vec, 1), jnp.float32)
+    curvature = jnp.zeros((vec, 1), jnp.float32)
+    for index in range(size):
+        image_proj = image_proj + dot(image_parts[index], panel_parts[index], 1, 1, FULL)
+        norm = norm + row_sum(rhs_parts[index], dir_parts[index])
+        curvature = curvature + row_sum(dir_parts[index], image_parts[index])
+    dot_sum[column, :, :rank] = image_proj
+    dot_sum[column, :, rank:] = pack([norm, curvature])
+    exchange("panel", dot_sum, 2)
+    totals = total_of(dot_sum, panel_size)
+    image_proj = totals[:, :rank]
+    norm, curvature = totals[:, rank : rank + 1], totals[:, rank + 1 : rank + 2]
+    step = norm / curvature
+    coef = dot(proj_ref[...] - step * image_proj, inverse_ref[...], 1, 0, FULL)
+    for index in range(size):
+        pre_parts[index] = precondition(
+            rhs_parts[index] - step * image_parts[index], coef, panel_parts[index]
+        )
+    second_sum[column] = tile_product(pre_parts)
+    exchange("panel", second_sum, 3)
+    resid_own = rhs_own[...] - step * image_own
+    pre_own = precondition(resid_own, coef, panel_own[...])
+    pre_image = total_of(second_sum, panel_size) + noise * pre_own
+    last_sum[row] = pack(
+        [
+            row_sum(resid_own, pre_own),
+            row_sum(pre_own, pre_image),
+            row_sum(pre_own, image_own) + row_sum(dir_own, pre_image),
+        ]
+    )
+    exchange("blk", last_sum, 4)
+    totals = total_of(last_sum, size)
+    new_norm = totals[:, 0:1]
+    ratio = new_norm / norm
+    curvature = totals[:, 1:2] + ratio * (totals[:, 2:3] + ratio * curvature)
+    last = new_norm / curvature
+    solution_ref[...] = step * dir_own + last * (pre_own + ratio * dir_own)
+    residual_ref[...] = resid_own - last * (pre_image + ratio * image_own)
+
+
+def loop_of(proj, inverse, rhs_parts, rhs_own, panel_parts, panel_own, tile, noise):
+    size, vec, quarter = rhs_parts.shape
+    panel_size = lax.axis_size("panel")
+    rank = proj.shape[1]
+    rounded = lax.reduce_precision(tile, 8, 7)
+    high = rounded.astype(jnp.bfloat16)
+    low = (tile - rounded).astype(jnp.bfloat16)
+    most = max(size, panel_size)
+    own = jax.ShapeDtypeStruct(rhs_own.shape, jnp.float32)
+    return pl.pallas_call(
+        functools.partial(loop_kernel, size, panel_size, vec, quarter),
+        out_shape=[own, own],
+        in_specs=[VMEM] * 9,
+        out_specs=[VMEM] * 2,
+        scratch_shapes=[
+            pltpu.VMEM(rhs_parts.shape, jnp.float32),
+            pltpu.VMEM(rhs_parts.shape, jnp.float32),
+            pltpu.VMEM((panel_size,) + rhs_own.shape, jnp.float32),
+            pltpu.VMEM((panel_size,) + rhs_own.shape, jnp.float32),
+            pltpu.VMEM(rhs_parts.shape, jnp.float32),
+            pltpu.VMEM((panel_size, vec, rank + 128), jnp.float32),
+            pltpu.VMEM((size, vec, 128), jnp.float32),
+            pltpu.SemaphoreType.DMA((5, most)),
+            pltpu.SemaphoreType.DMA((5, most)),
+        ],
+        compiler_params=pltpu.CompilerParams(
+            collective_id=8, has_side_effects=True, vmem_limit_bytes=LOOP_BYTES
+        ),
+    )(proj, inverse, rhs_parts, rhs_own, panel_parts, panel_own, high, low, noise)
 
 
 def per_device(points, lengthscale, noise_level, right_sides, pivots):
@@ -194,7 +473,7 @@
     local_sq = jnp.sum(scaled * scaled, axis=0)
     row_ids = lax.axis_index("blk") * row_count + lax.iota(jnp.int32, row_count)
     onehot = (pivots[:, None] == row_ids[None, :]).astype(jnp.float32)
-    picked = dot(onehot, scaled, 1, 1)
+    picked = dot(onehot, scaled, 1, 1, FULL)
 
     def own_quarter(vectors):
         return lax.dynamic_slice_in_dim(vectors, panel_start, quarter, 1)
@@ -202,7 +481,7 @@
     def spread(stacked):
         return stacked.transpose(1, 0, 2).reshape(vec, -1)
 
-    quarter_points, picks, rhs_parts = gather(
+    quarter_points, picks, rhs_parts = forward_gather(
         [own_quarter(scaled).T, picked, own_quarter(right_sides)], "blk", 0
     )
     visit = quarter_points.reshape(-1, points.shape[0])
@@ -220,8 +499,17 @@
     gram, proj = sum_over([dot(panel_q, panel_q, 1, 1), dot(rhs_q, panel_q, 1, 1)], "panel", 2)
     inverse = inverse_of(noise * inner_kernel + gram)
 
+    if 4 * tile.size <= LOOP_BYTES // 3:
+        blocks = panel_q.reshape(panel_q.shape[0], -1, quarter).transpose(1, 0, 2)
+        return tuple(
+            loop_of(
+                proj, inverse, rhs_parts, right_sides, blocks, panel_own, tile,
+                noise_level.reshape(1, 1),
+            )
+        )
+
     def coefficients_of(projected):
-        return dot(projected, inverse, 1, 0)
+        return dot(projected, inverse, 1, 0, FULL)
 
     def precondition(resid, coefficients, panel_rows):
         return (resid - dot(coefficients, panel_rows, 1, 0)) / noise

time: 124 us -> 106 us (0.85)
  matrix products: 22.8 us -> 11 us
  Pallas kernels: 92.4 us -> 84 us
  local copies, waits for them, and re-layouts: 4.31 us -> 7.73 us
  other arithmetic: 2.78 us -> 1.32 us
    pallas_call x0 -> x2, Pallas kernels: none -> 58.2 us  [the longest x1 35.4 us: loop_of(): pl.pallas_call(functools.partial(loop_kernel, size, panel_size, vec, quar...]
    pallas_call x4 -> x1, Pallas kernels: 54.5 us -> 4.5 us  [gather(): pl.pallas_call(functools.partial(gather_kernel, axis, size, count), out_s...]
    pallas_call x4 -> x1, Pallas kernels: 27.3 us -> 10.7 us  [sum_over(): pl.pallas_call(functools.partial(sum_kernel, axis, steps, count), out_sha...]
    dot_general x16 -> x7, matrix products: 22.8 us -> 11 us  [dot(): lax.dot_general(left, right, (((left_dim,), (right_dim,)), ((), ())), pre...]
    reshape x0 -> x1, local copies, waits for them, and re-layouts: none -> 1.83 us  [per_device(): blocks = panel_q.reshape(panel_q.shape[0], -1, quarter).transpose(1, 0, 2)]
    exp x0 -> x1, local copies, waits for them, and re-layouts: none -> 1.63 us  [kern(): return jnp.exp(-0.5 * (left_sq[:, None] + right_sq[None, :] - 2.0 * cross))]
    unnamed x11 -> x13, local copies, waits for them, and re-layouts: 3.69 us -> 2.44 us
where the time goes in v3:
time: 106 us
  Pallas kernels  84 us (79%)
  matrix products  11 us (10%)
  local copies, waits for them, and re-layouts  7.73 us (7%)
  between operations  1.51 us (1%)
  other arithmetic  1.32 us (1%)
    pallas_call x1, Pallas kernels, loop_of(): pl.pallas_call(functools.partial(loop_kernel, size, panel_size, vec, quar...  35.4 us
    pallas_call x1, Pallas kernels, forward_gather(): pl.pallas_call(functools.partial(forward_kernel, axis, size, count), out_...  22.9 us
    dot_general x7, matrix products, dot(): lax.dot_general(left, right, (((left_dim,), (right_dim,)), ((), ())), pre...  11 us
    pallas_call x1, Pallas kernels, sum_over(): pl.pallas_call(functools.partial(sum_kernel, axis, steps, count), out_sha...  10.7 us
    pallas_call x1, Pallas kernels, inverse_of(): pl.pallas_call(functools.partial(inverse_kernel, side, 64, 8), out_shape=...  10.6 us
    pallas_call x1, Pallas kernels, gather(): pl.pallas_call(functools.partial(gather_kernel, axis, size, count), out_s...  4.5 us
    unnamed x13, local copies, waits for them, and re-layouts  2.44 us

profile of v3, /device:TPU:0, one launch (start us, length us, event | category | flops | bytes accessed | tf_op | source)
XLA Modules:
  0.0 105.6 jit_solution(17914396523494334204)
XLA Ops:
  0.6 0.0 copy-start.4
  1.3 0.9 constant_dynamic-slice_fusion.refs_2_
  2.2 1.2 %copy.8 = f32[128,768]{0,1:T(8,128)S(1)} copy(f32[128,768]{1,0:T(8,128)} %param.5) | data formatting | bytes 786432 | tf_op args[0]
  3.3 0.8 multiply_reduce_fusion.1
  4.2 0.0 copy-start.2
  4.2 0.0 copy-done.4
  4.2 0.3 fusion.12.refs_1_
  4.5 22.9 %shard_map.68 = (f32[8,192,128]{2,1,0:T(8,128)S(1)}, f32[8,64,128]{2,1,0:T(8,128)S(1)}, f32[8,17,192]{2,1,0:T(8,128)S(1)}) custom-call(f32[192,128]{1,0:T(8,128)S(1)} %dynamic-slice_bitcast_fusion.refs_0_, f32[64,128]{1,0:T(8,128)S(1)} %fusion.12.refs_1_, f32[17,192]{1,0:T(8,128)S(1)} %constant_dynamic-slice_fusion.refs_2_), custom_call_target="tpu_custom_call" | custom-call | tf_op jit(solution)/shard_map/pallas_call | solution.py:181
  27.4 0.0 copy-start
  27.4 0.4 multiply_reduce_fusion
  27.8 0.1 add.78
  27.9 4.5 %shard_map.69 = f32[4,64,128]{2,1,0:T(8,128)S(1)} custom-call(f32[64,128]{1,0:T(8,128)S(1)} %reduce_sum.36.refs_0_), custom_call_target="tpu_custom_call" | custom-call | tf_op jit(solution)/shard_map/pallas_call | solution.py:64
  32.4 0.1 multiply_reduce_fusion.2
  32.5 0.1 add.76
  32.6 0.8 reshape.38
  33.4 0.0 copy-done.2
  33.4 0.9 fusion.6.refs_5_
  34.3 0.0 copy-done
  34.3 0.0 copy-start.3
  34.3 1.6 %fusion.3 = f32[256,1536]{1,0:T(8,128)S(1)} fusion(f32[256,128]{1,0:T(8,128)S(1)} %bitcast.26, f32[1536,128]{1,0:T(8,128)S(1)} %bitcast.28, f32[1536]{0:T(1024)S(1)} %add.78, f32[256]{0:T(256)S(1)} %add.76), kind=kOutput, calls=%fused_computation.7 | convolution fusion | flops 605552640 | bytes 2497536 | tf_op jit(solution)/shard_map/dot_general | solution.py:18
  35.9 0.0 copy-done.3
  35.9 0.7 fusion.17.refs_1_
  36.7 0.8 fusion.16.refs_0_
  37.5 1.6 %copy.10 = f32[256,1536]{0,1:T(8,128)} copy(f32[256,1536]{1,0:T(8,128)S(1)} %fusion.3) | data formatting | bytes 3145728 | tf_op jit(solution)/shard_map/exp | solution.py:298
  39.2 10.7 %shard_map.70 = (f32[256,256]{1,0:T(8,128)S(1)}, f32[17,256]{1,0:T(8,128)S(1)}) custom-call(f32[256,256]{1,0:T(8,128)S(1)} %fusion.16.refs_0_, f32[17,256]{1,0:T(8,128)S(1)} %fusion.17.refs_1_), custom_call_target="tpu_custom_call" | custom-call | tf_op jit(solution)/shard_map/pallas_call | solution.py:229
  49.8 0.4 fusion.11.a_ref
  50.3 10.6 %shard_map.71.refs_1_ = f32[256,256]{1,0:T(8,128)S(1)} custom-call(f32[256,256]{1,0:T(8,128)S(1)} %fusion.11.a_ref), custom_call_target="tpu_custom_call" | custom-call | tf_op jit(solution)/shard_map/pallas_call | solution.py:287
  60.9 1.8 %copy.11 = f32[256,8,192]{2,0,1:T(8,128)S(1)} copy(f32[256,8,192]{0,2,1:T(8,128)} %bitcast.31) | data formatting | bytes 3145728 | tf_op jit(solution)/shard_map/reshape | solution.py:503
  62.7 0.0 copy-start.1
  62.8 6.2 %fusion = (bf16[1536,768]{1,0:T(8,128)(2,1)S(1)}, bf16[1536,768]{1,0:T(8,128)(2,1)S(1)}) fusion(f32[1536,128]{1,0:T(8,128)} %bitcast.29, f32[128,768]{0,1:T(8,128)} %copy-done.2, f32[768]{0:T(1024)S(1)} %get-tuple-element.12, f32[1536]{0:T(1024)S(1)} %add.78), kind=kOutput, calls=%fused_computation.2 | convolution fusion | flops 1821376512 | bytes 5907456 | tf_op jit(solution)/shard_map/dot_general | solution.py:18
  69.0 0.0 copy-done.1
  69.0 35.4 %shard_map.72 = (f32[17,768]{1,0:T(8,128)S(1)}, f32[17,768]{1,0:T(8,128)S(1)}) custom-call(f32[17,256]{1,0:T(8,128)S(1)} %get-tuple-element.10.refs_0_, f32[256,256]{1,0:T(8,128)S(1)} %shard_map.71.refs_1_, f32[8,17,192]{2,1,0:T(8,128)S(1)} %get-tuple-element.9.refs_2_, f32[17,768]{1,0:T(8,128)S(1)} %copy-done.1, f32[8,256,192]{2,1,0:T(8,128)S(1)} %bitcast.24, ...), custom_call_target="tpu_custom_call" | custom-call | tf_op jit(solution)/shard_map/pallas_call | solution.py:443
  104.4 0.6 copy.15
  105.0 0.6 copy.16
  (4 shorter events, 0.1 us)
Async XLA Ops:
  0.6 3.5 %copy-start.4 = (s32[64]{0:T(128)S(1)}, s32[64]{0:T(128)}, u32[]{:S(2)}) copy-start(s32[64]{0:T(128)} %param.9) | copy-start | bytes 772
  4.2 29.2 %copy-start.2 = (f32[128,768]{0,1:T(8,128)}, f32[128,768]{0,1:T(8,128)S(1)}, u32[]{:S(2)}) copy-start(f32[128,768]{0,1:T(8,128)S(1)} %get-tuple-element.13) | copy-start | bytes 1179652
  27.4 6.9 %copy-start = (f32[8,192,128]{2,1,0:T(8,128)}, f32[8,192,128]{2,1,0:T(8,128)S(1)}, u32[]{:S(2)}) copy-start(f32[8,192,128]{2,1,0:T(8,128)S(1)} %get-tuple-element.8) | copy-start | bytes 2359300
  34.3 1.7 %copy-start.3 = (f32[17,1536]{1,0:T(8,128)S(1)}, f32[17,1536]{1,0:T(8,128)}, u32[]{:S(2)}) copy-start(f32[17,1536]{1,0:T(8,128)} %reshape.38) | copy-start | bytes 313348
  62.7 6.2 %copy-start.1 = (f32[17,768]{1,0:T(8,128)S(1)}, f32[17,768]{1,0:T(8,128)}, u32[]{:S(2)}) copy-start(f32[17,768]{1,0:T(8,128)} %refs_3_.1) | copy-start | bytes 156676

commit v4 on v3

--- a/solution.py
+++ b/solution.py
@@ -190,10 +190,31 @@
     )(*arrays)
 
 
-def sum_kernel(axis, steps, count, *refs):
-    ins, outs = refs[:count], refs[count : 2 * count]
-    landed = refs[2 * count : 3 * count]
-    send_sem, recv_sem = refs[3 * count :]
+def tile_rows(refs, first, last, chunk):
+    visit_ref, scaled_ref, sq_ref, high_ref, low_ref = refs
+
+    def one(index, carry):
+        rows = pl.ds(pl.multiple_of(index * chunk, 16), chunk)
+        left = visit_ref[rows, :]
+        cross = dot(left, scaled_ref[...], 1, 0, FULL)
+        left_sq = jnp.sum(left * left, axis=1, keepdims=True)
+        values = jnp.exp(-0.5 * (left_sq + sq_ref[...] - 2.0 * cross))
+        high = values.astype(jnp.bfloat16)
+        high_ref[rows, :] = high
+        low_ref[rows, :] = (values - high.astype(jnp.float32)).astype(jnp.bfloat16)
+        return carry
+
+    lax.fori_loop(first, last, one, 0)
+
+
+def sum_kernel(axis, steps, count, chunk, *refs):
+    extra = 3 if chunk else 0
+    ins, outs = refs[:count], refs[count + extra : 2 * count + extra]
+    made = 2 * count + extra
+    tile_refs = refs[count : count + extra] + refs[made : made + (2 if chunk else 0)]
+    refs = refs[made + (2 if chunk else 0) :]
+    landed = refs[:count]
+    send_sem, recv_sem = refs[count:]
     me = lax.axis_index(axis)
     partners = [me + s * (1 - 2 * lax.rem(me // s, 2)) for s in steps]
     barrier = pltpu.get_barrier_semaphore()
@@ -214,23 +235,31 @@
             )
             copy.start()
             copies.append(copy)
+        if chunk:
+            pieces = tile_refs[0].shape[0] // chunk
+            cut = [pieces * (step + i) // len(steps) for i in (0, 1)]
+            tile_rows(tile_refs, cut[0], cut[1], chunk)
         for item in range(count):
             copies[item].wait()
             outs[item][...] = held[item][...] + landed[item][step]
             held[item] = outs[item]
 
 
-def sum_over(arrays, axis, collective_id):
+def sum_over(arrays, axis, collective_id, tile_of=(), chunk=0):
     size = lax.axis_size(axis)
     steps = []
     while (1 << len(steps)) < size:
         steps.append(1 << len(steps))
     count = len(arrays)
+    halves = []
+    if chunk:
+        shape = (tile_of[0].shape[0], tile_of[1].shape[1])
+        halves = [jax.ShapeDtypeStruct(shape, jnp.bfloat16)] * 2
     return pl.pallas_call(
-        functools.partial(sum_kernel, axis, steps, count),
-        out_shape=[jax.ShapeDtypeStruct(a.shape, a.dtype) for a in arrays],
-        in_specs=[VMEM] * count,
-        out_specs=[VMEM] * count,
+        functools.partial(sum_kernel, axis, steps, count, chunk),
+        out_shape=[jax.ShapeDtypeStruct(a.shape, a.dtype) for a in arrays] + halves,
+        in_specs=[VMEM] * (count + len(tile_of)),
+        out_specs=[VMEM] * (count + len(halves)),
         scratch_shapes=[pltpu.VMEM((len(steps),) + a.shape, a.dtype) for a in arrays]
         + [
             pltpu.SemaphoreType.DMA((count, len(steps))),
@@ -239,7 +268,7 @@
         compiler_params=pltpu.CompilerParams(
             collective_id=collective_id, has_side_effects=True, vmem_limit_bytes=VMEM_BYTES
         ),
-    )(*arrays)
+    )(*arrays, *tile_of)
 
 
 def inverse_kernel(side, part, width, a_ref, out_ref):
@@ -299,10 +328,10 @@
 
 
 def loop_kernel(size, panel_size, vec, quarter, *refs):
-    proj_ref, inverse_ref, rhs_parts, rhs_own, panel_parts, panel_own = refs[:6]
+    proj_ref, inverse_ref, rhs_visit, rhs_own, panel_visit, panel_own = refs[:6]
     high_ref, low_ref, noise_ref, solution_ref, residual_ref = refs[6:11]
-    dir_parts, pre_parts, first_sum, second_sum, image_parts, dot_sum, last_sum = refs[11:18]
-    send_sem, recv_sem = refs[18:]
+    first_sum, second_sum, image_parts, dot_sum, last_sum = refs[11:16]
+    send_sem, recv_sem = refs[16:]
     row, column = lax.axis_index("blk"), lax.axis_index("panel")
     rank = proj_ref.shape[1]
     barrier = pltpu.get_barrier_semaphore()
@@ -348,20 +377,17 @@
     def precondition(resid, coefficients, panel_rows):
         return (resid - dot(coefficients, panel_rows, 1, 0, FULL)) / noise
 
-    def tile_product(parts):
+    def tile_product(vectors):
+        high = vectors.astype(jnp.bfloat16)
+        low = (vectors - high.astype(jnp.float32)).astype(jnp.bfloat16)
         product = jnp.zeros(rhs_own.shape, jnp.float32)
-        for index in range(size):
-            rows = pl.ds(index * quarter, quarter)
-            part = parts[index]
-            high = part.astype(jnp.bfloat16)
-            low = (part - high.astype(jnp.float32)).astype(jnp.bfloat16)
-            for left, right in ((high, high_ref), (low, high_ref), (high, low_ref)):
-                product = product + lax.dot_general(
-                    left,
-                    right[rows, :],
-                    (((1,), (0,)), ((), ())),
-                    preferred_element_type=jnp.float32,
-                )
+        for left, right in ((high, high_ref), (low, high_ref), (high, low_ref)):
+            product = product + lax.dot_general(
+                left,
+                right[...],
+                (((1,), (0,)), ((), ())),
+                preferred_element_type=jnp.float32,
+            )
         return product
 
     def row_sum(left, right):
@@ -376,9 +402,8 @@
         return packed
 
     coef = dot(proj_ref[...], inverse_ref[...], 1, 0, FULL)
-    for index in range(size):
-        dir_parts[index] = precondition(rhs_parts[index], coef, panel_parts[index])
-    first_sum[column] = tile_product(dir_parts)
+    dir_visit = precondition(rhs_visit[...], coef, panel_visit[...])
+    first_sum[column] = tile_product(dir_visit)
     pl.semaphore_wait(barrier, size + panel_size - 2)
     exchange("panel", first_sum, 0)
     dir_own = precondition(rhs_own[...], coef, panel_own[...])
@@ -390,13 +415,10 @@
             image_parts[row] = image_own[:, index * quarter : (index + 1) * quarter]
 
     exchange("blk", image_parts, 1)
-    image_proj = jnp.zeros((vec, rank), jnp.float32)
-    norm = jnp.zeros((vec, 1), jnp.float32)
-    curvature = jnp.zeros((vec, 1), jnp.float32)
-    for index in range(size):
-        image_proj = image_proj + dot(image_parts[index], panel_parts[index], 1, 1, FULL)
-        norm = norm + row_sum(rhs_parts[index], dir_parts[index])
-        curvature = curvature + row_sum(dir_parts[index], image_parts[index])
+    image_visit = jnp.concatenate([image_parts[index] for index in range(size)], axis=1)
+    image_proj = dot(image_visit, panel_visit[...], 1, 1, FULL)
+    norm = row_sum(rhs_visit[...], dir_visit)
+    curvature = row_sum(dir_visit, image_visit)
     dot_sum[column, :, :rank] = image_proj
     dot_sum[column, :, rank:] = pack([norm, curvature])
     exchange("panel", dot_sum, 2)
@@ -405,11 +427,8 @@
     norm, curvature = totals[:, rank : rank + 1], totals[:, rank + 1 : rank + 2]
     step = norm / curvature
     coef = dot(proj_ref[...] - step * image_proj, inverse_ref[...], 1, 0, FULL)
-    for index in range(size):
-        pre_parts[index] = precondition(
-            rhs_parts[index] - step * image_parts[index], coef, panel_parts[index]
-        )
-    second_sum[column] = tile_product(pre_parts)
+    pre_visit = precondition(rhs_visit[...] - step * image_visit, coef, panel_visit[...])
+    second_sum[column] = tile_product(pre_visit)
     exchange("panel", second_sum, 3)
     resid_own = rhs_own[...] - step * image_own
     pre_own = precondition(resid_own, coef, panel_own[...])
@@ -431,13 +450,10 @@
     residual_ref[...] = resid_own - last * (pre_image + ratio * image_own)
 
 
-def loop_of(proj, inverse, rhs_parts, rhs_own, panel_parts, panel_own, tile, noise):
-    size, vec, quarter = rhs_parts.shape
-    panel_size = lax.axis_size("panel")
-    rank = proj.shape[1]
-    rounded = lax.reduce_precision(tile, 8, 7)
-    high = rounded.astype(jnp.bfloat16)
-    low = (tile - rounded).astype(jnp.bfloat16)
+def loop_of(proj, inverse, rhs_visit, rhs_own, panel_visit, panel_own, high, low, noise):
+    size, panel_size = lax.axis_size("blk"), lax.axis_size("panel")
+    vec, rank = proj.shape
+    quarter = rhs_visit.shape[1] // size
     most = max(size, panel_size)
     own = jax.ShapeDtypeStruct(rhs_own.shape, jnp.float32)
     return pl.pallas_call(
@@ -446,11 +462,9 @@
         in_specs=[VMEM] * 9,
         out_specs=[VMEM] * 2,
         scratch_shapes=[
-            pltpu.VMEM(rhs_parts.shape, jnp.float32),
-            pltpu.VMEM(rhs_parts.shape, jnp.float32),
             pltpu.VMEM((panel_size,) + rhs_own.shape, jnp.float32),
             pltpu.VMEM((panel_size,) + rhs_own.shape, jnp.float32),
-            pltpu.VMEM(rhs_parts.shape, jnp.float32),
+            pltpu.VMEM((size, vec, quarter), jnp.float32),
             pltpu.VMEM((panel_size, vec, rank + 128), jnp.float32),
             pltpu.VMEM((size, vec, 128), jnp.float32),
             pltpu.SemaphoreType.DMA((5, most)),
@@ -459,7 +473,7 @@
         compiler_params=pltpu.CompilerParams(
             collective_id=8, has_side_effects=True, vmem_limit_bytes=LOOP_BYTES
         ),
-    )(proj, inverse, rhs_parts, rhs_own, panel_parts, panel_own, high, low, noise)
+    )(proj, inverse, rhs_visit, rhs_own, panel_visit, panel_own, high, low, noise)
 
 
 def per_device(points, lengthscale, noise_level, right_sides, pivots):
@@ -494,19 +508,21 @@
     panel_q = kern(pivot_rows, pivot_sq, visit, 1, visit_sq)
     panel_own = kern(pivot_rows, pivot_sq, scaled, 0, local_sq)
     inner_kernel = kern(pivot_rows, pivot_sq, pivot_rows, 1, pivot_sq)
-    tile = kern(visit, visit_sq, scaled, 0, local_sq)
-
-    gram, proj = sum_over([dot(panel_q, panel_q, 1, 1), dot(rhs_q, panel_q, 1, 1)], "panel", 2)
-    inverse = inverse_of(noise * inner_kernel + gram)
-
-    if 4 * tile.size <= LOOP_BYTES // 3:
-        blocks = panel_q.reshape(panel_q.shape[0], -1, quarter).transpose(1, 0, 2)
+    sums = [dot(panel_q, panel_q, 1, 1), dot(rhs_q, panel_q, 1, 1)]
+    if 4 * visit.shape[0] * row_count <= LOOP_BYTES // 3:
+        gram, proj, high, low = sum_over(
+            sums, "panel", 2, (visit, scaled, local_sq[None, :]), quarter
+        )
+        inverse = inverse_of(noise * inner_kernel + gram)
         return tuple(
             loop_of(
-                proj, inverse, rhs_parts, right_sides, blocks, panel_own, tile,
+                proj, inverse, rhs_q, right_sides, panel_q, panel_own, high, low,
                 noise_level.reshape(1, 1),
             )
         )
+    tile = kern(visit, visit_sq, scaled, 0, local_sq)
+    gram, proj = sum_over(sums, "panel", 2)
+    inverse = inverse_of(noise * inner_kernel + gram)
 
     def coefficients_of(projected):
         return dot(projected, inverse, 1, 0, FULL)

time: 106 us -> 93.7 us (0.88)
  matrix products: 11 us -> 5.53 us
  local copies, waits for them, and re-layouts: 7.73 us -> 2.62 us
  Pallas kernels: 84 us -> 82.2 us
    dot_general x7 -> x6, matrix products: 11 us -> 5.53 us  [dot(): lax.dot_general(left, right, (((left_dim,), (right_dim,)), ((), ())), pre...]
    pallas_call x1, Pallas kernels: 35.4 us -> 32.4 us  [loop_of(): pl.pallas_call(functools.partial(loop_kernel, size, panel_size, vec, quar...]
    reshape x1 -> x0, local copies, waits for them, and re-layouts: 1.83 us -> none  [per_device(): blocks = panel_q.reshape(panel_q.shape[0], -1, quarter).transpose(1, 0, 2)]
    exp x1 -> x0, local copies, waits for them, and re-layouts: 1.63 us -> none  [kern(): return jnp.exp(-0.5 * (left_sq[:, None] + right_sq[None, :] - 2.0 * cross))]
    pallas_call x1, Pallas kernels: 10.7 us -> 11.9 us  [sum_over(): pl.pallas_call(functools.partial(sum_kernel, axis, steps, count, chunk),...]
    unnamed x13 -> x4, local copies, waits for them, and re-layouts: 2.44 us -> 1.27 us
where the time goes in v4:
time: 93.7 us; the launch traced here: 93.4 us
  Pallas kernels  82.2 us (88%)
  matrix products  5.53 us (6%)
  local copies, waits for them, and re-layouts  2.62 us (3%)
  other arithmetic  1.61 us (2%)
  between operations  1.48 us (2%)
    pallas_call x1, Pallas kernels, loop_of(): pl.pallas_call(functools.partial(loop_kernel, size, panel_size, vec, quar...  32.4 us
    pallas_call x1, Pallas kernels, forward_gather(): pl.pallas_call(functools.partial(forward_kernel, axis, size, count), out_...  22.9 us
    pallas_call x1, Pallas kernels, sum_over(): pl.pallas_call(functools.partial(sum_kernel, axis, steps, count, chunk),...  11.9 us
    pallas_call x1, Pallas kernels, inverse_of(): pl.pallas_call(functools.partial(inverse_kernel, side, 64, 8), out_shape=...  10.5 us
    dot_general x6, matrix products, dot(): lax.dot_general(left, right, (((left_dim,), (right_dim,)), ((), ())), pre...  5.53 us
    pallas_call x1, Pallas kernels, gather(): pl.pallas_call(functools.partial(gather_kernel, axis, size, count), out_s...  4.55 us

profile of v4, /device:TPU:0, one launch (start us, length us, event | category | flops | bytes accessed | tf_op | source)
XLA Modules:
  0.0 93.4 jit_solution(14832906675936043948)
XLA Ops:
  0.6 1.1 %multiply_reduce_fusion.1 = (f32[768]{0:T(1024)S(1)}, f32[128,768]{1,0:T(8,128)S(1)}) fusion(f32[128,768]{1,0:T(8,128)} %param.5, f32[128]{0:T(128)} %param.6), kind=kLoop, calls=%fused_computation.15 | loop fusion | flops 294144 | bytes 790016 | tf_op jit(solution)/shard_map/reduce_sum | solution.py:487
  1.8 0.1 dynamic-slice_bitcast_fusion
  1.9 0.1 copy.7.refs_0_
  2.0 0.9 constant_dynamic-slice_fusion.refs_2_
  2.8 1.0 %fusion.11.refs_1_ = f32[64,128]{1,0:T(8,128)S(1)} fusion(f32[128,768]{1,0:T(8,128)S(1)} %get-tuple-element.17.refs_3_, s32[768]{0:T(1024)S(1)} %iota_add_fusion, s32[64]{0:T(128)} %param.9), kind=kOutput, calls=%fused_computation.17 | convolution fusion | flops 75546624 | bytes 429312 | tf_op jit(solution)/shard_map/dot_general | solution.py:18
  3.9 22.9 %shard_map.68 = (f32[8,192,128]{2,1,0:T(8,128)S(1)}, f32[8,64,128]{2,1,0:T(8,128)S(1)}, f32[8,17,192]{2,1,0:T(8,128)S(1)}) custom-call(f32[192,128]{1,0:T(8,128)S(1)} %copy.7.refs_0_, f32[64,128]{1,0:T(8,128)S(1)} %fusion.11.refs_1_, f32[17,192]{1,0:T(8,128)S(1)} %constant_dynamic-slice_fusion.refs_2_), custom_call_target="tpu_custom_call" | custom-call | tf_op jit(solution)/shard_map/pallas_call | solution.py:181
  26.8 4.5 %shard_map.69 = f32[4,64,128]{2,1,0:T(8,128)S(1)} custom-call(f32[64,128]{1,0:T(8,128)S(1)} %reduce_sum.36.refs_0_), custom_call_target="tpu_custom_call" | custom-call | tf_op jit(solution)/shard_map/pallas_call | solution.py:64
  31.3 0.1 multiply_reduce_fusion.2
  31.5 0.1 add.63
  31.5 0.4 multiply_reduce_fusion
  31.9 0.1 add.65
  32.0 1.6 %fusion.2.refs_4_ = f32[256,1536]{1,0:T(8,128)S(1)} fusion(f32[256,128]{1,0:T(8,128)S(1)} %bitcast.22, f32[1536,128]{1,0:T(8,128)S(1)} %bitcast.20, f32[1536]{0:T(1024)S(1)} %add.65, f32[256]{0:T(256)S(1)} %add.63), kind=kOutput, calls=%fused_computation.3 | convolution fusion | flops 605552640 | bytes 2497536 | tf_op jit(solution)/shard_map/dot_general | solution.py:18
  33.7 0.1 reshape.33.refs_2_
  33.8 0.7 fusion.16.refs_1_
  34.5 0.8 fusion.15.refs_0_
  35.4 11.9 %shard_map.70 = (f32[256,256]{1,0:T(8,128)S(1)}, f32[17,256]{1,0:T(8,128)S(1)}, bf16[1536,768]{1,0:T(8,128)(2,1)S(1)}, bf16[1536,768]{1,0:T(8,128)(2,1)S(1)}) custom-call(f32[256,256]{1,0:T(8,128)S(1)} %fusion.15.refs_0_, f32[17,256]{1,0:T(8,128)S(1)} %fusion.16.refs_1_, f32[1536,128]{1,0:T(8,128)S(1)} %bitcast.21, ...), custom_call_target="tpu_custom_call" | custom-call | tf_op jit(solution)/shard_map/pallas_call | solution.py:258
  47.3 0.0 copy-start
  48.0 0.4 fusion.10.a_ref
  48.4 10.5 %shard_map.71.refs_1_ = f32[256,256]{1,0:T(8,128)S(1)} custom-call(f32[256,256]{1,0:T(8,128)S(1)} %fusion.10.a_ref), custom_call_target="tpu_custom_call" | custom-call | tf_op jit(solution)/shard_map/pallas_call | solution.py:316
  58.9 0.9 fusion.5.refs_5_
  59.8 0.0 copy-done
  59.8 32.4 %shard_map.72 = (f32[17,768]{1,0:T(8,128)S(1)}, f32[17,768]{1,0:T(8,128)S(1)}) custom-call(f32[17,256]{1,0:T(8,128)S(1)} %get-tuple-element.12.refs_0_, f32[256,256]{1,0:T(8,128)S(1)} %shard_map.71.refs_1_, f32[17,1536]{1,0:T(8,128)S(1)} %reshape.33.refs_2_, f32[17,768]{1,0:T(8,128)S(1)} %copy-done, f32[256,1536]{1,0:T(8,128)S(1)} %fusion.2.refs_4_, ...), custom_call_target="tpu_custom_call" | custom-call | tf_op jit(solution)/shard_map/pallas_call | solution.py:459
  92.2 0.6 copy.12
  92.8 0.6 copy.13
  (4 shorter events, 0.1 us)
Async XLA Ops:
  47.3 12.5 %copy-start = (f32[17,768]{1,0:T(8,128)S(1)}, f32[17,768]{1,0:T(8,128)}, u32[]{:S(2)}) copy-start(f32[17,768]{1,0:T(8,128)} %refs_3_.1) | copy-start | bytes 156676

commit v5 on v4

--- a/solution.py
+++ b/solution.py
@@ -348,7 +348,7 @@
         )
     noise = noise_ref[...]
 
-    def exchange(axis, buffer, phase):
+    def exchange(axis, buffer, phase, beside=None):
         me, count = (row, size) if axis == "blk" else (column, panel_size)
 
         def copy_of(hop, slot):
@@ -363,10 +363,12 @@
 
         for hop in range(count - 1, 0, -1):
             copy_of(hop, me).start()
+        result = beside() if beside else None
         for hop in range(1, count):
             copy_of(hop, lax.rem(me + count - hop, count)).wait_recv()
         for hop in range(1, count):
             copy_of(hop, me).wait_send()
+        return result
 
     def total_of(buffer, count):
         total = buffer[0]
@@ -405,8 +407,9 @@
     dir_visit = precondition(rhs_visit[...], coef, panel_visit[...])
     first_sum[column] = tile_product(dir_visit)
     pl.semaphore_wait(barrier, size + panel_size - 2)
-    exchange("panel", first_sum, 0)
-    dir_own = precondition(rhs_own[...], coef, panel_own[...])
+    dir_own = exchange(
+        "panel", first_sum, 0, lambda: precondition(rhs_own[...], coef, panel_own[...])
+    )
     image_own = total_of(first_sum, panel_size) + noise * dir_own
     for index in range(panel_size):
 
@@ -429,9 +432,10 @@
     coef = dot(proj_ref[...] - step * image_proj, inverse_ref[...], 1, 0, FULL)
     pre_visit = precondition(rhs_visit[...] - step * image_visit, coef, panel_visit[...])
     second_sum[column] = tile_product(pre_visit)
-    exchange("panel", second_sum, 3)
     resid_own = rhs_own[...] - step * image_own
-    pre_own = precondition(resid_own, coef, panel_own[...])
+    pre_own = exchange(
+        "panel", second_sum, 3, lambda: precondition(resid_own, coef, panel_own[...])
+    )
     pre_image = total_of(second_sum, panel_size) + noise * pre_own
     last_sum[row] = pack(
         [

time: 93.7 us -> 92.3 us (0.985)
  Pallas kernels: 82.2 us -> 80.8 us
    pallas_call x1, Pallas kernels: 32.4 us -> 31 us  [loop_of(): pl.pallas_call(functools.partial(loop_kernel, size, panel_size, vec, quar...]
where the time goes in v5:
time: 92.3 us; the launch traced here: 92 us
  Pallas kernels  80.8 us (88%)
  matrix products  5.53 us (6%)
  local copies, waits for them, and re-layouts  2.62 us (3%)
  other arithmetic  1.61 us (2%)
  between operations  1.48 us (2%)
    pallas_call x1, Pallas kernels, loop_of(): pl.pallas_call(functools.partial(loop_kernel, size, panel_size, vec, quar...  31 us
    pallas_call x1, Pallas kernels, forward_gather(): pl.pallas_call(functools.partial(forward_kernel, axis, size, count), out_...  22.9 us
    pallas_call x1, Pallas kernels, sum_over(): pl.pallas_call(functools.partial(sum_kernel, axis, steps, count, chunk),...  11.9 us
    pallas_call x1, Pallas kernels, inverse_of(): pl.pallas_call(functools.partial(inverse_kernel, side, 64, 8), out_shape=...  10.5 us
    dot_general x6, matrix products, dot(): lax.dot_general(left, right, (((left_dim,), (right_dim,)), ((), ())), pre...  5.53 us
    pallas_call x1, Pallas kernels, gather(): pl.pallas_call(functools.partial(gather_kernel, axis, size, count), out_s...  4.55 us

profile of v5, /device:TPU:0, one launch (start us, length us, event | category | flops | bytes accessed | tf_op | source)
XLA Modules:
  0.0 92.0 jit_solution(11930223111252990953)
XLA Ops:
  0.6 1.1 %multiply_reduce_fusion.1 = (f32[768]{0:T(1024)S(1)}, f32[128,768]{1,0:T(8,128)S(1)}) fusion(f32[128,768]{1,0:T(8,128)} %param.5, f32[128]{0:T(128)} %param.6), kind=kLoop, calls=%fused_computation.15 | loop fusion | flops 294144 | bytes 790016 | tf_op jit(solution)/shard_map/reduce_sum | solution.py:491
  1.8 0.1 dynamic-slice_bitcast_fusion
  1.9 0.1 copy.7.refs_0_
  2.0 0.9 constant_dynamic-slice_fusion.refs_2_
  2.8 1.0 %fusion.11.refs_1_ = f32[64,128]{1,0:T(8,128)S(1)} fusion(f32[128,768]{1,0:T(8,128)S(1)} %get-tuple-element.17.refs_3_, s32[768]{0:T(1024)S(1)} %iota_add_fusion, s32[64]{0:T(128)} %param.9), kind=kOutput, calls=%fused_computation.17 | convolution fusion | flops 75546624 | bytes 429312 | tf_op jit(solution)/shard_map/dot_general | solution.py:18
  3.9 22.9 %shard_map.68 = (f32[8,192,128]{2,1,0:T(8,128)S(1)}, f32[8,64,128]{2,1,0:T(8,128)S(1)}, f32[8,17,192]{2,1,0:T(8,128)S(1)}) custom-call(f32[192,128]{1,0:T(8,128)S(1)} %copy.7.refs_0_, f32[64,128]{1,0:T(8,128)S(1)} %fusion.11.refs_1_, f32[17,192]{1,0:T(8,128)S(1)} %constant_dynamic-slice_fusion.refs_2_), custom_call_target="tpu_custom_call" | custom-call | tf_op jit(solution)/shard_map/pallas_call | solution.py:181
  26.8 4.5 %shard_map.69 = f32[4,64,128]{2,1,0:T(8,128)S(1)} custom-call(f32[64,128]{1,0:T(8,128)S(1)} %reduce_sum.36.refs_0_), custom_call_target="tpu_custom_call" | custom-call | tf_op jit(solution)/shard_map/pallas_call | solution.py:64
  31.3 0.1 multiply_reduce_fusion.2
  31.5 0.1 add.63
  31.5 0.4 multiply_reduce_fusion
  31.9 0.1 add.65
  32.0 1.6 %fusion.2.refs_4_ = f32[256,1536]{1,0:T(8,128)S(1)} fusion(f32[256,128]{1,0:T(8,128)S(1)} %bitcast.22, f32[1536,128]{1,0:T(8,128)S(1)} %bitcast.20, f32[1536]{0:T(1024)S(1)} %add.65, f32[256]{0:T(256)S(1)} %add.63), kind=kOutput, calls=%fused_computation.3 | convolution fusion | flops 605552640 | bytes 2497536 | tf_op jit(solution)/shard_map/dot_general | solution.py:18
  33.7 0.1 reshape.33.refs_2_
  33.8 0.7 fusion.16.refs_1_
  34.5 0.8 fusion.15.refs_0_
  35.4 11.9 %shard_map.70 = (f32[256,256]{1,0:T(8,128)S(1)}, f32[17,256]{1,0:T(8,128)S(1)}, bf16[1536,768]{1,0:T(8,128)(2,1)S(1)}, bf16[1536,768]{1,0:T(8,128)(2,1)S(1)}) custom-call(f32[256,256]{1,0:T(8,128)S(1)} %fusion.15.refs_0_, f32[17,256]{1,0:T(8,128)S(1)} %fusion.16.refs_1_, f32[1536,128]{1,0:T(8,128)S(1)} %bitcast.21, ...), custom_call_target="tpu_custom_call" | custom-call | tf_op jit(solution)/shard_map/pallas_call | solution.py:258
  47.3 0.0 copy-start
  48.0 0.4 fusion.10.a_ref
  48.4 10.5 %shard_map.71.refs_1_ = f32[256,256]{1,0:T(8,128)S(1)} custom-call(f32[256,256]{1,0:T(8,128)S(1)} %fusion.10.a_ref), custom_call_target="tpu_custom_call" | custom-call | tf_op jit(solution)/shard_map/pallas_call | solution.py:316
  58.9 0.9 fusion.5.refs_5_
  59.8 0.0 copy-done
  59.8 31.0 %shard_map.72 = (f32[17,768]{1,0:T(8,128)S(1)}, f32[17,768]{1,0:T(8,128)S(1)}) custom-call(f32[17,256]{1,0:T(8,128)S(1)} %get-tuple-element.12.refs_0_, f32[256,256]{1,0:T(8,128)S(1)} %shard_map.71.refs_1_, f32[17,1536]{1,0:T(8,128)S(1)} %reshape.33.refs_2_, f32[17,768]{1,0:T(8,128)S(1)} %copy-done, f32[256,1536]{1,0:T(8,128)S(1)} %fusion.2.refs_4_, ...), custom_call_target="tpu_custom_call" | custom-call | tf_op jit(solution)/shard_map/pallas_call | solution.py:463
  90.8 0.6 copy.12
  91.4 0.6 copy.13
  (4 shorter events, 0.1 us)
Async XLA Ops:
  47.3 12.5 %copy-start = (f32[17,768]{1,0:T(8,128)S(1)}, f32[17,768]{1,0:T(8,128)}, u32[]{:S(2)}) copy-start(f32[17,768]{1,0:T(8,128)} %refs_3_.1) | copy-start | bytes 156676
